TPU v7x, 256 devices: a whole 4x4x8 slice. The times are simulated.
256 devices in a mesh: depth: 32 (over y, z), rows: 8 (over x, core).
Axes of the slice: x: 4, y: 4, z: 8, core: 2. Of those that a mesh axis runs over, the one named last changes fastest.
Arguments:
- field: bfloat16 [512, 512, 1024], P('depth', 'rows'), may hold values from -6 to 6
- tf_centers: float32 [4], replicated, may hold values from -1.5 to 1.5
- tf_widths: float32 [4], replicated, may hold values from 0.4 to 1.2
- tf_density: float32 [4], replicated, may hold values from 0.5 to 4
- tf_colors: float32 [3, 4], replicated, may hold values from 0.1 to 1
- light: float32 [3], replicated, may hold values from 0.5 to 1.5
Outputs:
- image: float32 [4, 512, 1024], P(None, 'rows', 'depth')
All inputs are finite; a program needn't handle non-finite values.
Results may differ from a plain program's by a relative error of at most 0.0003.
Values may be sent and summed in bfloat16 or wider, within the bound.
No kernel may reach another device: no remote copies, remote signals or barrier semaphores. Data moves between devices by JAX's collectives and lax.ppermute only.
A program may use at most 64 MiB of HBM per device.

v0:
```python
import jax
import jax.numpy as jnp
from jax import lax
from jax.sharding import PartitionSpec as P


def padded_2(block, sides, width):
    for axis, dim in sides:
        count = lax.axis_size(axis)
        forward = [(i, i + 1) for i in range(count - 1)]
        backward = [(target, source) for source, target in forward]
        low = lax.ppermute(
            lax.slice_in_dim(block, block.shape[dim] - width, None, axis=dim), axis, forward
        )
        high = lax.ppermute(lax.slice_in_dim(block, 0, width, axis=dim), axis, backward)
        block = jnp.concatenate([low, block, high], axis=dim)
    return block


def carried_in(part, axis, combine, identity):
    place = lax.axis_index(axis)
    gathered = lax.all_gather(part, axis)
    state = jnp.zeros_like(part) + jnp.asarray(identity, part.dtype)

    def one(hop, state):
        return combine(state, lax.dynamic_index_in_dim(gathered, hop, 0, False))

    return lax.fori_loop(0, place, one, state)


def shade_cells(padded, tf_centers, tf_widths, tf_density, tf_colors, light, step_size):
    values = padded[1:-1, 1:-1, 1:-1]
    grad_z = (padded[2:, 1:-1, 1:-1] - padded[:-2, 1:-1, 1:-1]) * 0.5
    grad_y = (padded[1:-1, 2:, 1:-1] - padded[1:-1, :-2, 1:-1]) * 0.5
    grad_x = (padded[1:-1, 1:-1, 2:] - padded[1:-1, 1:-1, :-2]) * 0.5
    grad_sq = grad_z * grad_z + grad_y * grad_y + grad_x * grad_x
    light_dir = light / jnp.sqrt(jnp.sum(light * light))
    facing = jnp.abs(grad_z * light_dir[0] + grad_y * light_dir[1] + grad_x * light_dir[2])
    lighting = 0.3 + 0.7 * facing / jnp.sqrt(grad_sq + 1.0)
    sigma = jnp.zeros_like(values)
    bump_total = jnp.zeros_like(values)
    colour_red = jnp.zeros_like(values)
    colour_green = jnp.zeros_like(values)
    colour_blue = jnp.zeros_like(values)
    for bump_index in range(tf_centers.shape[0]):
        scaled = (values - tf_centers[bump_index]) / tf_widths[bump_index]
        bump = jnp.exp(-scaled * scaled)
        sigma = sigma + tf_density[bump_index] * bump
        bump_total = bump_total + bump
        colour_red = colour_red + tf_colors[0, bump_index] * bump
        colour_green = colour_green + tf_colors[1, bump_index] * bump
        colour_blue = colour_blue + tf_colors[2, bump_index] * bump
    factor = lighting / (bump_total + 0.1)
    emit = jnp.stack([colour_red * factor, colour_green * factor, colour_blue * factor], 0)
    depth_tau = sigma * (0.25 + grad_sq / (grad_sq + 1.0)) * step_size
    return (depth_tau, emit)


def compose_local(depth_tau, emit):
    before = jnp.cumsum(depth_tau, 0) - depth_tau
    weight_z = jnp.exp(-before) * (1.0 - jnp.exp(-depth_tau))
    colour_sum = jnp.sum(weight_z[None] * emit, axis=1)
    return (colour_sum, jnp.sum(depth_tau, 0))


def add_depths(earlier, later):
    return earlier + later


def shards(field, tf_centers, tf_widths, tf_density, tf_colors, light):
    depth_count = lax.axis_size("depth")
    step_size = 0.5 / (field.shape[0] * depth_count)
    extended = padded_2(field, (("depth", 0), ("rows", 1)), 1)
    padded = jnp.pad(extended, ((0, 0), (0, 0), (1, 1))).astype(jnp.float32)
    depth_tau, emit = shade_cells(
        padded, tf_centers, tf_widths, tf_density, tf_colors, light, step_size
    )
    colour_sum, tau_total = compose_local(depth_tau, emit)
    front_tau = carried_in(tau_total, "depth", add_depths, jnp.zeros_like(tau_total))
    shaded = colour_sum * jnp.exp(-front_tau)[None]
    stacked = jnp.concatenate([shaded, tau_total[None]], 0)
    summed = lax.psum_scatter(stacked, "depth", scatter_dimension=2, tiled=True)
    image = jnp.concatenate([summed[:3], (1.0 - jnp.exp(-summed[3]))[None]], 0)
    return image


def solution(mesh):
    placed = (P("depth", "rows", None), P(), P(), P(), P(), P())
    return jax.shard_map(
        shards, mesh=mesh, in_specs=placed, out_specs=P(None, "rows", "depth"), check_vma=False
    )
```

profile of v0, /device:TPU:2, one launch (start us, length us, event | category | flops | bytes accessed | tf_op | source)
XLA Modules:
  0.0 344.4 jit_solution(4557722021318292419)
XLA Ops:
  6.5 0.0 all-gather.3.cloned.1.call-start
  6.5 1.0 fusion.22
  7.5 3.8 %collective-permute-start = (bf16[1,64,1024]{2,1,0:T(8,128)(2,1)S(1)}, bf16[1,64,1024]{2,1,0:T(8,128)(2,1)S(1)}, u32[]{:S(2)}, u32[]{:S(2)}) collective-permute-start(bf16[1,64,1024]{2,1,0:T(8,128)(2,1)S(1)} %get-tuple-element.50), channel_id=1, source_target_pairs={{0,8},{8,16},{16,24},{24,32},{32,40},{40,48},{48,56},{56,64},{64,7... | collective-permute-start | bytes 393224 | tf_op jit(solution)/shard_map/ppermute | solution.py:12
  11.4 1.3 collective-permute-start.1
  12.7 1.5 fusion.26
  14.2 1.4 fusion.27
  15.6 0.0 collective-permute-done
  15.6 1.8 constant_dynamic-update-slice_fusion.1
  17.4 1.0 collective-permute-done.1
  18.4 0.1 fusion.21
  18.5 1.9 collective-permute-start.2
  20.5 3.6 %collective-permute-start.3 = (bf16[18,1,1024]{2,1,0:T(2,128)(2,1)S(1)}, bf16[18,1,1024]{2,1,0:T(2,128)(2,1)S(1)}, u32[]{:S(2)}, u32[]{:S(2)}) collective-permute-start(bf16[18,1,1024]{2,1,0:T(2,128)(2,1)S(1)} %get-tuple-element.48), channel_id=1, source_target_pairs={{1,0},{2,1},{3,2},{4,3},{5,4},{6,5},{7,6},{9,8},{10,9},{11,10},{12... | collective-permute-start | bytes 110600 | tf_op jit(solution)/shard_map/ppermute | solution.py:15
  24.1 0.0 copy-done.3
  24.1 0.7 fusion.25
  24.8 0.0 collective-permute-done.2
  24.8 1.3 collective-permute-done.3
  26.1 2.4 fusion.17
  28.5 0.0 copy-start
  28.5 0.0 copy-start.4
  28.5 0.0 copy-start.2
  28.5 19.4 %fusion.19 = (f32[64,1024]{1,0:T(8,128)}, f32[16,64,1024]{2,1,0:T(8,128)}) fusion(f32[18,66,1026]{2,1,0:T(8,128)S(1)} %fusion.17, f32[]{:T(128)} %bitcast.12, f32[]{:T(128)} %bitcast.11, f32[]{:T(128)} %bitcast.10, f32[]{:T(128)} %bitcast.9, f32[]{:T(128)} %bitcast.8, f32[]{:T(128)} %bitcast.7, f32[]{:T(128)} %bitcast.6, f32[]{:T(128)} %bitcast.5, ...), kind=kLoop, calls=%fused_computation.48 | loop fusion | flops 41877504 | bytes 33816624 | tf_op jit(solution)/shard_map/reduce_sum | solution.py:63
  48.0 0.0 copy-done
  48.0 0.0 all-gather.3.cloned.1.call-update
  48.0 0.0 all-reduce.4.cloned.1.call-start
  48.0 0.0 copy-done.4
  48.0 0.7 multiply_reduce_fusion
  49.5 0.7 fusion.24
  52.1 0.0 copy-done.2
  52.1 0.7 fusion.23
  52.8 4.7 %subtract_multiply_fusion = f32[16,64,1024]{2,1,0:T(8,128)S(1)} fusion(f32[16,64,1024]{2,1,0:T(8,128)} %get-tuple-element.44), kind=kOutput, calls=%fused_computation.28 | output fusion | flops 20971520 | bytes 8388608 | tf_op jit(solution)/shard_map/jit(cumsum)/reduce_window_sum | solution.py:60
  57.5 0.0 slice-done
  57.5 0.5 slice-done.1
  58.0 19.4 %multiply_bitcast_fusion.2 = (f32[1,16,64,1024]{3,2,1,0:T(8,128)S(1)}, f32[16,64,1024]{2,1,0:T(8,128)S(1)}) fusion(f32[]{:T(128)} %bitcast.16, f32[]{:T(128)} %bitcast.15, f32[]{:T(128)} %bitcast.14, f32[]{:T(128)} %bitcast.13, f32[]{:T(128)} %bitcast.12, f32[]{:T(128)} %bitcast.11, f32[18,66,1026]{2,1,0:T(8,128)S(1)} %bitcast.44, f32[]{:T(128)} %bitcast.9, ...), kind=kLoop, calls=%fused_computation.27 | loop fusion | flops 52428800 | bytes 37748796 | tf_op jit(solution)/shard_map/stack | solution.py:54
  77.5 16.2 %multiply_bitcast_fusion.1 = (f32[1,16,64,1024]{3,2,1,0:T(8,128)S(1)}, f32[1,16,64,1024]{3,2,1,0:T(8,128)S(1)}) fusion(f32[16,64,1024]{2,1,0:T(8,128)S(1)} %get-tuple-element.42, f32[]{:T(128)} %bitcast.24, f32[]{:T(128)} %bitcast.23, f32[]{:T(128)} %bitcast.22, f32[]{:T(128)} %bitcast.21, f32[]{:T(128)} %bitcast.12, f32[]{:T(128)} %bitcast.11, ...), kind=kLoop, calls=%fused_computation.26 | loop fusion | flops 33554432 | bytes 16777280 | tf_op jit(solution)/shard_map/stack | solution.py:54
  93.6 2.0 fusion
  95.6 0.0 copy-start.1
  95.6 55.9 %all-gather.3.cloned.1.call-done = f32[2048,1024]{1,0:T(8,128)} async-done(((f32[64,1024]{1,0:T(8,128)}), f32[2048,1024]{1,0:T(8,128)}) %all-gather.3.cloned.1.call-update) | async-done | bytes 8388624 | tf_op jit(solution)/shard_map/all_gather | solution.py:22
  151.6 0.0 copy-start.5
  151.6 0.1 broadcast_multiply_fusion
  151.7 0.0 copy-done.1
  151.7 0.1 pad_maximum_fusion
  151.8 1.8 copy.14
  153.6 0.0 all-reduce.4.cloned.1.call-update
  153.6 0.6 dynamic-slice
  154.9 180.3 %all-reduce.4.cloned.1.call-done = f32[4,64,1024]{1,0,2:T(4,128)} async-done(((f32[4,64,1024]{1,0,2:T(4,128)}), f32[4,64,1024]{1,0,2:T(4,128)}) %all-reduce.4.cloned.1.call-update) | async-done | bytes 1048592
  335.2 0.9 constant_dynamic-slice_fusion.1
  336.1 0.9 constant_dynamic-slice_fusion
  337.0 0.6 copy.17
  (13 shorter events, 0.2 us)
Async XLA Ops:
  6.5 17.6 %copy-start.3 = (f32[4]{0:T(128)S(1)}, f32[4]{0:T(128)}, u32[]{:S(2)}) copy-start(f32[4]{0:T(128)} %param.11) | copy-start | bytes 52
  6.5 145.0 %all-gather.3.cloned.1.call-start = ((), (), s32[]{:S(2)}) async-start(), calls=%async_computation | async-start | bytes 8650752 | tf_op jit(solution)/shard_map/all_gather | solution.py:22
  7.5 8.1 %collective-permute-start = (bf16[1,64,1024]{2,1,0:T(8,128)(2,1)S(1)}, bf16[1,64,1024]{2,1,0:T(8,128)(2,1)S(1)}, u32[]{:S(2)}, u32[]{:S(2)}) collective-permute-start(bf16[1,64,1024]{2,1,0:T(8,128)(2,1)S(1)} %get-tuple-element.50), channel_id=1, source_target_pairs={{0,8},{8,16},{16,24},{24,32},{32,40},{40,48},{48,56},{56,64},{64,7... | collective-permute-start | bytes 393224 | tf_op jit(solution)/shard_map/ppermute | solution.py:12
  11.4 7.0 %collective-permute-start.1 = (bf16[1,64,1024]{2,1,0:T(8,128)(2,1)S(1)}, bf16[1,64,1024]{2,1,0:T(8,128)(2,1)S(1)}, u32[]{:S(2)}, u32[]{:S(2)}) collective-permute-start(bf16[1,64,1024]{2,1,0:T(8,128)(2,1)S(1)} %get-tuple-element.49), channel_id=1, source_target_pairs={{8,0},{16,8},{24,16},{32,24},{40,32},{48,40},{56,48},{64,56},{72,6... | collective-permute-start | bytes 393224 | tf_op jit(solution)/shard_map/ppermute | solution.py:15
  18.5 6.3 %collective-permute-start.2 = (bf16[18,1,1024]{2,1,0:T(2,128)(2,1)S(1)}, bf16[18,1,1024]{2,1,0:T(2,128)(2,1)S(1)}, u32[]{:S(2)}, u32[]{:S(2)}) collective-permute-start(bf16[18,1,1024]{2,1,0:T(2,128)(2,1)S(1)} %get-tuple-element.47), channel_id=1, source_target_pairs={{0,1},{1,2},{2,3},{3,4},{4,5},{5,6},{6,7},{8,9},{9,10},{10,11},{11... | collective-permute-start | bytes 110600 | tf_op jit(solution)/shard_map/ppermute | solution.py:12
  20.5 5.6 %collective-permute-start.3 = (bf16[18,1,1024]{2,1,0:T(2,128)(2,1)S(1)}, bf16[18,1,1024]{2,1,0:T(2,128)(2,1)S(1)}, u32[]{:S(2)}, u32[]{:S(2)}) collective-permute-start(bf16[18,1,1024]{2,1,0:T(2,128)(2,1)S(1)} %get-tuple-element.48), channel_id=1, source_target_pairs={{1,0},{2,1},{3,2},{4,3},{5,4},{6,5},{7,6},{9,8},{10,9},{11,10},{12... | collective-permute-start | bytes 110600 | tf_op jit(solution)/shard_map/ppermute | solution.py:15
  28.5 19.5 %copy-start = (f32[18,66,1026]{2,1,0:T(8,128)}, f32[18,66,1026]{2,1,0:T(8,128)S(1)}, u32[]{:S(2)}) copy-start(f32[18,66,1026]{2,1,0:T(8,128)S(1)} %fusion.17) | copy-start | bytes 14626660
  28.5 19.6 %copy-start.4 = (f32[3]{0:T(128)S(1)}, f32[3]{0:T(128)}, u32[]{:S(2)}) copy-start(f32[3]{0:T(128)} %param.13) | copy-start | bytes 40
  28.5 23.6 %copy-start.2 = (f32[3,4]{1,0:T(4,128)S(1)}, f32[3,4]{1,0:T(4,128)}, u32[]{:S(2)}) copy-start(f32[3,4]{1,0:T(4,128)} %param.12) | copy-start | bytes 148
  48.0 287.2 %all-reduce.4.cloned.1.call-start = ((), (), s32[]{:S(2)}) async-start(), calls=%async_computation.1 | async-start | bytes 4194304
  52.8 4.7 %slice-start = ((s8[5971968]{0:T(1024)(128)(4,1)}), s8[4194304]{0:T(1024)(128)(4,1)S(1)}, s32[]{:S(2)}) async-start(s8[5971968]{0:T(1024)(128)(4,1)} %bitcast.43), calls=%async_computation.2 | async-start | bytes 8388608
  52.8 5.2 %slice-start.1 = ((s8[5971968]{0:T(1024)(128)(4,1)}), s8[1777664]{0:T(1024)(128)(4,1)S(1)}, s32[]{:S(2)}) async-start(s8[5971968]{0:T(1024)(128)(4,1)} %bitcast.43), calls=%async_computation.3 | async-start | bytes 3555328
  95.6 56.1 %copy-start.1 = (f32[64,1024]{1,0:T(8,128)S(1)}, f32[64,1024]{1,0:T(8,128)}, u32[]{:S(2)}) copy-start(f32[64,1024]{1,0:T(8,128)} %get-tuple-element.43) | copy-start | bytes 786436
  151.6 2.0 copy-start.5
Sparse Core Ops, SparseCore 0:
  48.1 103.3 all-gather.2
  155.0 180.1 all-reduce.3
where the time goes:
time: 346 us; the launch traced here: 344 us
  waiting for transfers between devices  239 us (69%)
  other arithmetic  65 us (19%)
  between operations  17 us (5%)
  local copies, waits for them, and re-layouts  13.1 us (4%)
  starting transfers between devices  10.7 us (3%)
    unnamed x3, waiting for transfers between devices  180 us
    all_gather x1, waiting for transfers between devices, carried_in(): gathered = lax.all_gather(part, axis)  55.9 us
    another operation x2, other arithmetic, shade_cells(): jnp.stack([colour_red * factor, colour_green * factor, colour_blue * fact...  35.6 us
    reduce_sum x1, other arithmetic, compose_local(): return (colour_sum, jnp.sum(depth_tau, 0))  19.4 us
  transfers between devices with their start and end apart: 6, of which 4 were waited for; matrix products, arithmetic and copies ran while one was open for 15% of the time, Pallas kernels for 0%

commit v1 on v0

v1 whole, which is shorter than its diff:
```python
import math

import jax
import jax.numpy as jnp
from jax import lax
from jax.experimental import pallas as pl
from jax.experimental.pallas import tpu as pltpu
from jax.sharding import PartitionSpec as P

LOG2E = math.log2(math.e)
TILE_ROWS = 16


def shade_kernel(
    step_size, centers, widths, density, colors, light,
    field, plane_lo, plane_hi, row_lo, row_hi,
    out, cells, slope_x, rays,
):
    depth, rows, width = field.shape
    lanes = width // 128

    lane = lax.broadcasted_iota(jnp.int32, (TILE_ROWS, 128), 1)

    def spread(plane, first, tile):
        for j in range(lanes):
            cells[j, plane, pl.ds(8 + first, TILE_ROWS), :] = tile[:, 128 * j : 128 * (j + 1)]

    def prepare(index, carry):
        plane = index // (rows // TILE_ROWS)
        first = pl.multiple_of((index % (rows // TILE_ROWS)) * TILE_ROWS, TILE_ROWS)
        tile = field[plane, pl.ds(first, TILE_ROWS), :].astype(jnp.float32)
        spread(plane + 1, first, tile)
        left = pltpu.roll(tile, 1, 1)
        right = pltpu.roll(tile, width - 1, 1)
        for j in range(lanes):
            before, after = left[:, 128 * j : 128 * (j + 1)], right[:, 128 * j : 128 * (j + 1)]
            if j == 0:
                before = jnp.where(lane == 0, 0.0, before)
            if j == lanes - 1:
                after = jnp.where(lane == 127, 0.0, after)
            slope_x[j, plane, pl.ds(first, TILE_ROWS), :] = after - before
        return carry

    lax.fori_loop(0, depth * (rows // TILE_ROWS), prepare, 0)
    for first in range(0, rows, TILE_ROWS):
        spread(0, first, plane_lo[first : first + TILE_ROWS, :].astype(jnp.float32))
        spread(depth + 1, first, plane_hi[first : first + TILE_ROWS, :].astype(jnp.float32))
    low, high = row_lo[...].astype(jnp.float32), row_hi[...].astype(jnp.float32)
    for j in range(lanes):
        for plane in range(depth):
            cells[j, plane + 1, 7:8, :] = low[plane : plane + 1, 128 * j : 128 * (j + 1)]
            cells[j, plane + 1, 8 + rows : 9 + rows, :] = high[plane : plane + 1, 128 * j : 128 * (j + 1)]

    def full(scalar):
        return jnp.full((TILE_ROWS, 128), scalar, jnp.float32)

    count = centers.shape[0]
    center = [full(centers[k]) for k in range(count)]
    sharp = [-LOG2E / (full(widths[k]) * full(widths[k])) for k in range(count)]
    dense = [full(density[k]) * (-4.0 * LOG2E * step_size) for k in range(count)]
    lights = [full(light[k]) for k in range(3)]
    length = lax.rsqrt(lights[0] * lights[0] + lights[1] * lights[1] + lights[2] * lights[2])
    lights = [component * length * 0.7 for component in lights]

    def march(index, carry):
        j = index // (rows // TILE_ROWS)
        first = (index % (rows // TILE_ROWS)) * TILE_ROWS
        here = pl.ds(pl.multiple_of(first + 8, 8), TILE_ROWS)
        previous, current = cells[j, 0, here, :], cells[j, 1, here, :]
        total = jnp.zeros((TILE_ROWS, 128), jnp.float32)
        clear = jnp.ones((TILE_ROWS, 128), jnp.float32)
        sums = [jnp.zeros((TILE_ROWS, 128), jnp.float32) for _ in range(count)]
        for plane in range(depth):
            following = cells[j, plane + 2, here, :]
            dz = following - previous
            dy = cells[j, plane + 1, pl.ds(first + 9, TILE_ROWS), :] - cells[j, plane + 1, pl.ds(first + 7, TILE_ROWS), :]
            dx = slope_x[j, plane, pl.ds(pl.multiple_of(first, TILE_ROWS), TILE_ROWS), :]
            root = lax.rsqrt(dz * dz + dy * dy + dx * dx + 4.0)
            lighting = 0.3 + jnp.abs(dz * lights[0] + dy * lights[1] + dx * lights[2]) * root
            bumps = []
            for k in range(count):
                offset = current - center[k]
                bumps.append(jnp.exp2(offset * offset * sharp[k]))
            sigma = dense[0] * bumps[0]
            weight = bumps[0] + 0.1
            for k in range(1, count):
                sigma = sigma + dense[k] * bumps[k]
                weight = weight + bumps[k]
            total = total + sigma * (0.3125 - root * root)
            remaining = jnp.exp2(total)
            factor = (clear - remaining) * lighting * pl.reciprocal(weight, approx=False)
            sums = [s + factor * b for s, b in zip(sums, bumps)]
            previous, current, clear = current, following, remaining
        kept = pl.ds(pl.multiple_of(first, TILE_ROWS), TILE_ROWS)
        for c in range(3):
            colour = colors[c, 0] * sums[0]
            for k in range(1, count):
                colour = colour + colors[c, k] * sums[k]
            rays[j, c, kept, :] = colour
        rays[j, 3, kept, :] = total
        return carry

    lax.fori_loop(0, lanes * (rows // TILE_ROWS), march, 0)

    def pack(j, carry):
        for c in range(4):
            tiles = [rays[j, c, 16 * q : 16 * (q + 1), :] for q in range(4)]
            for band in range(4):
                picked = None
                for q in range(4):
                    shift = (32 * (q - band)) % 128
                    moved = pltpu.roll(tiles[q], shift, 1) if shift else tiles[q]
                    picked = moved if q == 0 else jnp.where(lane >= 32 * q, moved, picked)
                out[4 * j + band, 16 * c : 16 * (c + 1), :] = picked
        return carry

    lax.fori_loop(0, lanes, pack, 0)


def compose_kernel(bricks, out):
    count = bricks.shape[0]
    total = jnp.zeros((16, 128), jnp.float32)
    image = [jnp.zeros((16, 128), jnp.float32) for _ in range(3)]
    for brick in range(count):
        front = jnp.exp2(total)
        for c in range(3):
            image[c] = image[c] + front * bricks[brick, 16 * c : 16 * (c + 1), :]
        total = total + bricks[brick, 48:64, :]
    image.append(1.0 - jnp.exp2(total))
    for c in range(4):
        turned = image[c].T
        out[c] = jnp.concatenate([turned[32 * q : 32 * (q + 1), :] for q in range(4)], axis=1)


def shards(field, tf_centers, tf_widths, tf_density, tf_colors, light):
    depth_count, row_count = lax.axis_size("depth"), lax.axis_size("rows")
    depth, rows, width = field.shape
    step_size = 0.5 / (depth * depth_count)

    def around(low_source, high_source, axis, count):
        up = [(i, i + 1) for i in range(count - 1)]
        down = [(i + 1, i) for i in range(count - 1)]
        return lax.ppermute(low_source, axis, up), lax.ppermute(high_source, axis, down)

    plane_lo, plane_hi = around(field[-1], field[0], "depth", depth_count)
    row_lo, row_hi = around(field[:, -1], field[:, 0], "rows", row_count)

    smem = pl.BlockSpec(memory_space=pltpu.SMEM)
    vmem = pl.BlockSpec(memory_space=pltpu.VMEM)
    lanes = width // 128
    bricks = pl.pallas_call(
        lambda *refs: shade_kernel(step_size, *refs),
        out_shape=jax.ShapeDtypeStruct((width // 32, rows, 128), jnp.float32),
        in_specs=[smem] * 5 + [vmem] * 5,
        out_specs=vmem,
        scratch_shapes=[
            pltpu.VMEM((lanes, depth + 2, rows + 16, 128), jnp.float32),
            pltpu.VMEM((lanes, depth, rows, 128), jnp.float32),
            pltpu.VMEM((lanes, 4, rows, 128), jnp.float32),
        ],
        compiler_params=pltpu.CompilerParams(vmem_limit_bytes=40 * 1024 * 1024),
        name="shade",
    )(tf_centers, tf_widths, tf_density, tf_colors, light, field, plane_lo, plane_hi, row_lo, row_hi)
    bricks = lax.all_to_all(bricks, "depth", 0, 0, tiled=True)
    image = pl.pallas_call(
        compose_kernel,
        out_shape=jax.ShapeDtypeStruct((4, width // depth_count, rows), jnp.float32),
        in_specs=[vmem],
        out_specs=vmem,
        name="compose",
    )(bricks)
    return jnp.transpose(image, (0, 2, 1))


def solution(mesh):
    placed = (P("depth", "rows", None), P(), P(), P(), P(), P())
    return jax.shard_map(
        shards, mesh=mesh, in_specs=placed, out_specs=P(None, "rows", "depth"), check_vma=False
    )
```

time: 346 us -> 82.5 us (0.24)
  the two profiles are of different devices: /device:TPU:2 before, /device:TPU:1 now
where the time goes in v1:
time: 82.5 us; the launch traced here: 82.1 us
  blocking collectives  39.4 us (48%)
  Pallas kernels  20 us (24%)
  starting transfers between devices  12.3 us (15%)
  local copies, waits for them, and re-layouts  7.04 us (9%)
  waiting for transfers between devices  3.29 us (4%)
    all_to_all x1, blocking collectives, shards(): bricks = lax.all_to_all(bricks, 'depth', 0, 0, tiled=True)  39.4 us
    pallas_call x1, Pallas kernels, shards(): pl.pallas_call(lambda *refs: shade_kernel(step_size, *refs), out_shape=ja...  17.8 us
    ppermute x2, starting transfers between devices, around(): lax.ppermute(low_source, axis, up)  9.06 us
    unnamed x14, local copies, waits for them, and re-layouts  4.92 us
    ppermute x2, waiting for transfers between devices, around(): lax.ppermute(high_source, axis, down)  3.29 us
    ppermute x2, starting transfers between devices, around(): lax.ppermute(high_source, axis, down)  3.22 us
    pallas_call x1, Pallas kernels, shards(): pl.pallas_call(compose_kernel, out_shape=jax.ShapeDtypeStruct((4, width /...  2.13 us
  transfers between devices with their start and end apart: 4, of which 1 were waited for; matrix products, arithmetic and copies ran while one was open for 1% of the time, Pallas kernels for 0%

profile of v1, /device:TPU:1, one launch (start us, length us, event | category | flops | bytes accessed | tf_op | source)
XLA Modules:
  0.0 82.1 jit_solution(17472776522298739545)
XLA Ops:
  0.0 1.0 %slice_bitcast_fusion = (bf16[64,1024]{1,0:T(8,128)(2,1)S(1)}, bf16[64,1024]{1,0:T(8,128)(2,1)S(1)}) fusion(bf16[16,64,1024]{2,1,0:T(8,128)(2,1)} %refs_5_.1), kind=kLoop, calls=%fused_computation | loop fusion | bytes 524288 | tf_op jit(solution)/shard_map/squeeze | solution.py:145
  1.0 1.3 %collective-permute-start.1 = (bf16[64,1024]{1,0:T(8,128)(2,1)S(1)}, bf16[64,1024]{1,0:T(8,128)(2,1)S(1)}, u32[]{:S(2)}, u32[]{:S(2)}) collective-permute-start(bf16[64,1024]{1,0:T(8,128)(2,1)S(1)} %get-tuple-element.7), channel_id=1, source_target_pairs={{8,0},{16,8},{24,16},{32,24},{40,32},{48,40},{56,48},{64,56},{72,6... | collective-permute-start | bytes 393224 | tf_op jit(solution)/shard_map/ppermute | solution.py:143
  2.3 5.0 %collective-permute-start = (bf16[64,1024]{1,0:T(8,128)(2,1)S(1)}, bf16[64,1024]{1,0:T(8,128)(2,1)S(1)}, u32[]{:S(2)}, u32[]{:S(2)}) collective-permute-start(bf16[64,1024]{1,0:T(8,128)(2,1)S(1)} %get-tuple-element.8), channel_id=1, source_target_pairs={{0,8},{8,16},{16,24},{24,32},{32,40},{40,48},{48,56},{56,64},{64,7... | collective-permute-start | bytes 393224 | tf_op jit(solution)/shard_map/ppermute | solution.py:143
  7.3 1.1 %fusion = (bf16[16,1,1024]{2,1,0:T(2,128)(2,1)S(1)}, bf16[16,1,1024]{2,1,0:T(2,128)(2,1)S(1)}) fusion(bf16[16,64,1024]{2,1,0:T(8,128)(2,1)} %refs_5_.1), kind=kLoop, calls=%fused_computation.4 | loop fusion | bytes 131072 | tf_op jit(solution)/shard_map/slice | solution.py:146
  8.5 4.1 %collective-permute-start.2 = (bf16[16,1024]{1,0:T(8,128)(2,1)S(1)}, bf16[16,1024]{1,0:T(8,128)(2,1)S(1)}, u32[]{:S(2)}, u32[]{:S(2)}) collective-permute-start(bf16[16,1024]{1,0:T(8,128)(2,1)S(1)} %bitcast.11), channel_id=1, source_target_pairs={{0,1},{1,2},{2,3},{3,4},{4,5},{5,6},{6,7},{8,9},{9,10},{10,11},{11... | collective-permute-start | bytes 98312 | tf_op jit(solution)/shard_map/ppermute | solution.py:143
  12.6 1.9 %collective-permute-start.3 = (bf16[16,1024]{1,0:T(8,128)(2,1)S(1)}, bf16[16,1024]{1,0:T(8,128)(2,1)S(1)}, u32[]{:S(2)}, u32[]{:S(2)}) collective-permute-start(bf16[16,1024]{1,0:T(8,128)(2,1)S(1)} %bitcast.12), channel_id=1, source_target_pairs={{1,0},{2,1},{3,2},{4,3},{5,4},{6,5},{7,6},{9,8},{10,9},{11,10},{12... | collective-permute-start | bytes 98312 | tf_op jit(solution)/shard_map/ppermute | solution.py:143
  14.5 0.0 collective-permute-done.2.refs_8_
  14.5 3.3 %collective-permute-done.3.refs_9_ = bf16[16,1024]{1,0:T(8,128)(2,1)S(1)} collective-permute-done((bf16[16,1024]{1,0:T(8,128)(2,1)S(1)}, bf16[16,1024]{1,0:T(8,128)(2,1)S(1)}, u32[]{:S(2)}, u32[]{:S(2)}) %collective-permute-start.3) | collective-permute-done | bytes 32800 | tf_op jit(solution)/shard_map/ppermute | solution.py:143
  17.8 0.0 collective-permute-done.1.refs_7_
  17.8 0.0 collective-permute-done.refs_6_
  17.8 0.0 copy-start
  17.8 1.6 %copy-done = bf16[16,64,1024]{2,1,0:T(8,128)(2,1)S(1)} copy-done((bf16[16,64,1024]{2,1,0:T(8,128)(2,1)S(1)}, bf16[16,64,1024]{2,1,0:T(8,128)(2,1)}, u32[]{:S(2)}) %copy-start) | copy-done | bytes 2097176
  19.4 0.0 copy-start.1
  19.4 0.7 copy-done.1
  20.1 0.0 copy-start.2
  20.1 0.7 copy-done.2
  20.7 0.0 copy-start.3
  20.7 0.7 copy-done.3
  21.4 0.0 copy-start.4
  21.4 0.7 copy-done.4
  22.0 0.0 copy-start.5
  22.0 0.7 copy-done.5
  22.7 17.8 %shade.1 = f32[32,64,128]{2,1,0:T(8,128)S(1)} custom-call(f32[4]{0:T(128)S(1)} %copy-done.2, f32[4]{0:T(128)S(1)} %copy-done.3, f32[4]{0:T(128)S(1)} %copy-done.4, f32[3,4]{1,0:T(4,128)S(1)} %copy-done.1, f32[3]{0:T(128)S(1)} %copy-done.5, bf16[16,64,1024]{2,1,0:T(8,128)(2,1)S(1)} %copy-done, bf16[64,1024]{1,0:T(8,128)(2,1)S(1)} %collective-permute-done.refs_6_, ...), custom_call_target="tpu_custom_call" | custom-call | tf_op jit(solution)/shard_map/shade/pallas_call | solution.py:151
  40.5 39.4 %all_to_all.5.bricks = f32[32,64,128]{2,1,0:T(8,128)} all-to-all(f32[32,64,128]{2,1,0:T(8,128)S(1)} %shade.1), channel_id=1, replica_groups=mesh['depth'=32,'rows'=8] {'depth'}, dimensions={0} | all-to-all | bytes 2097152 | tf_op jit(solution)/shard_map/all_to_all | solution.py:164
  79.9 2.1 %compose.1 = f32[4,32,64]{2,1,0:T(8,128)} custom-call(f32[32,64,128]{2,1,0:T(8,128)} %all_to_all.5.bricks), custom_call_target="tpu_custom_call" | custom-call | tf_op jit(solution)/shard_map/compose/pallas_call | solution.py:165
  (2 shorter events, 0.0 us)
Async XLA Ops:
  1.0 16.8 %collective-permute-start.1 = (bf16[64,1024]{1,0:T(8,128)(2,1)S(1)}, bf16[64,1024]{1,0:T(8,128)(2,1)S(1)}, u32[]{:S(2)}, u32[]{:S(2)}) collective-permute-start(bf16[64,1024]{1,0:T(8,128)(2,1)S(1)} %get-tuple-element.7), channel_id=1, source_target_pairs={{8,0},{16,8},{24,16},{32,24},{40,32},{48,40},{56,48},{64,56},{72,6... | collective-permute-start | bytes 393224 | tf_op jit(solution)/shard_map/ppermute | solution.py:143
  2.3 15.5 %collective-permute-start = (bf16[64,1024]{1,0:T(8,128)(2,1)S(1)}, bf16[64,1024]{1,0:T(8,128)(2,1)S(1)}, u32[]{:S(2)}, u32[]{:S(2)}) collective-permute-start(bf16[64,1024]{1,0:T(8,128)(2,1)S(1)} %get-tuple-element.8), channel_id=1, source_target_pairs={{0,8},{8,16},{16,24},{24,32},{32,40},{40,48},{48,56},{56,64},{64,7... | collective-permute-start | bytes 393224 | tf_op jit(solution)/shard_map/ppermute | solution.py:143
  8.5 6.0 %collective-permute-start.2 = (bf16[16,1024]{1,0:T(8,128)(2,1)S(1)}, bf16[16,1024]{1,0:T(8,128)(2,1)S(1)}, u32[]{:S(2)}, u32[]{:S(2)}) collective-permute-start(bf16[16,1024]{1,0:T(8,128)(2,1)S(1)} %bitcast.11), channel_id=1, source_target_pairs={{0,1},{1,2},{2,3},{3,4},{4,5},{5,6},{6,7},{8,9},{9,10},{10,11},{11... | collective-permute-start | bytes 98312 | tf_op jit(solution)/shard_map/ppermute | solution.py:143
  12.6 5.2 %collective-permute-start.3 = (bf16[16,1024]{1,0:T(8,128)(2,1)S(1)}, bf16[16,1024]{1,0:T(8,128)(2,1)S(1)}, u32[]{:S(2)}, u32[]{:S(2)}) collective-permute-start(bf16[16,1024]{1,0:T(8,128)(2,1)S(1)} %bitcast.12), channel_id=1, source_target_pairs={{1,0},{2,1},{3,2},{4,3},{5,4},{6,5},{7,6},{9,8},{10,9},{11,10},{12... | collective-permute-start | bytes 98312 | tf_op jit(solution)/shard_map/ppermute | solution.py:143
  17.8 1.6 %copy-start = (bf16[16,64,1024]{2,1,0:T(8,128)(2,1)S(1)}, bf16[16,64,1024]{2,1,0:T(8,128)(2,1)}, u32[]{:S(2)}) copy-start(bf16[16,64,1024]{2,1,0:T(8,128)(2,1)} %refs_5_.1) | copy-start | bytes 6291460
  19.4 0.7 copy-start.1
  20.1 0.7 copy-start.2
  20.7 0.7 copy-start.3
  21.4 0.7 copy-start.4
  22.0 0.7 copy-start.5

commit v2 on v1

v2 whole, which is shorter than its diff:
```python
import math

import jax
import jax.numpy as jnp
from jax import lax
from jax.experimental import pallas as pl
from jax.experimental.pallas import tpu as pltpu
from jax.sharding import PartitionSpec as P

LOG2E = math.log2(math.e)
TILE = 16
LANES = 128
BAND = 32
MB = 1024 * 1024


def dither(brick, shape):
    lane = lax.broadcasted_iota(jnp.int32, shape, 1)
    row = lax.broadcasted_iota(jnp.int32, shape, 0)
    phase = (lane * 29 + row * 13 + brick * 37) & 63
    return phase.astype(jnp.float32) * (1.0 / 64.0) + 1.0


def edges_kernel(field, first, last, row_first, row_last, tiles, gathered, sems):
    depth, rows, _ = field.shape
    copies = [
        pltpu.make_async_copy(field.at[:, 0:TILE], tiles.at[0], sems.at[0]),
        pltpu.make_async_copy(field.at[:, rows - TILE : rows], tiles.at[1], sems.at[1]),
        pltpu.make_async_copy(field.at[0], first, sems.at[2]),
        pltpu.make_async_copy(field.at[depth - 1], last, sems.at[3]),
    ]
    for copy in copies:
        copy.start()
    for side, (row, out) in enumerate(((0, row_first), (TILE - 1, row_last))):
        copies[side].wait()
        for plane in range(depth):
            tile = tiles[side, plane].astype(jnp.float32)
            gathered[side, plane : plane + 1, :] = tile[row : row + 1, :]
        out[...] = gathered[side].astype(jnp.bfloat16)
    copies[2].wait()
    copies[3].wait()


def shade_kernel(
    step_size, depth_count, row_count,
    centers_hbm, widths_hbm, density_hbm, colors_hbm, light_hbm, field_hbm,
    plane_lo, plane_hi, row_lo, row_hi,
    out, field, cells, rays, centers, widths, density, colors, light, field_sems, sems,
):
    depth, rows, width = field.shape
    lanes, tiles = width // LANES, rows // TILE

    chunks = field_sems.shape[0]
    chunk = depth // chunks
    loads = [
        pltpu.make_async_copy(
            field_hbm.at[pl.ds(c * chunk, chunk)], field.at[pl.ds(c * chunk, chunk)], field_sems.at[c]
        )
        for c in range(chunks)
    ]
    smalls = [
        pltpu.make_async_copy(source, target, sems.at[i])
        for i, (source, target) in enumerate(
            (
                (centers_hbm, centers), (widths_hbm, widths), (density_hbm, density),
                (colors_hbm, colors), (light_hbm, light),
            )
        )
    ]
    for copy in loads + smalls:
        copy.start()

    def spread(plane, first, tile):
        for j in range(lanes):
            cells[j + 1, plane, pl.ds(8 + first, TILE), :] = tile[:, LANES * j : LANES * (j + 1)]

    me, row_me = lax.axis_index("depth"), lax.axis_index("rows")
    keep_lo = (me > 0).astype(jnp.float32)
    keep_hi = (me < depth_count - 1).astype(jnp.float32)
    keep_up = (row_me > 0).astype(jnp.float32)
    keep_down = (row_me < row_count - 1).astype(jnp.float32)
    for first in range(0, rows, TILE):
        spread(0, first, plane_lo[first : first + TILE, :].astype(jnp.float32) * keep_lo)
        spread(depth + 1, first, plane_hi[first : first + TILE, :].astype(jnp.float32) * keep_hi)
    low, high = row_lo[...].astype(jnp.float32) * keep_up, row_hi[...].astype(jnp.float32) * keep_down
    for j in range(lanes):
        for plane in range(depth):
            cells[j + 1, plane + 1, 7:8, :] = low[plane : plane + 1, LANES * j : LANES * (j + 1)]
            cells[j + 1, plane + 1, 8 + rows : 9 + rows, :] = high[plane : plane + 1, LANES * j : LANES * (j + 1)]
    for side in (0, lanes + 1):
        for plane in range(depth):
            cells[side, plane + 1, 8 : 8 + rows, :] = jnp.zeros((rows, LANES), jnp.float32)

    def prepare(index, carry):
        plane = index // tiles
        first = pl.multiple_of((index % tiles) * TILE, TILE)
        spread(plane + 1, first, field[plane, pl.ds(first, TILE), :].astype(jnp.float32))
        return carry

    for c in range(chunks):
        loads[c].wait()
        lax.fori_loop(c * chunk * tiles, (c + 1) * chunk * tiles, prepare, 0)
    for copy in smalls:
        copy.wait()

    def full(scalar):
        return jnp.full((TILE, LANES), scalar, jnp.float32)

    count = centers.shape[0]
    center = [full(centers[k]) for k in range(count)]
    sharp = [-LOG2E / (full(widths[k]) * full(widths[k])) for k in range(count)]
    dense = [full(density[k]) * (-4.0 * LOG2E * step_size) for k in range(count)]
    lights = [full(light[k]) for k in range(3)]
    length = lax.rsqrt(lights[0] * lights[0] + lights[1] * lights[1] + lights[2] * lights[2])
    lights = [component * length * 0.7 for component in lights]

    lane = lax.broadcasted_iota(jnp.int32, (TILE, LANES), 1)
    at_first, at_last = lane == 0, lane == LANES - 1
    upper, odd = lane >= 64, (lane & 32) > 0
    scale = dither(me, (TILE, LANES)) * 65536.0

    def pack(j, c):
        def exchange(a, b, mask, shift):
            moved = pltpu.roll(jnp.where(mask, a, b), shift, 1)
            return jnp.where(mask, moved, a), jnp.where(mask, b, moved)

        part = [rays[j & 1, c, TILE * q : TILE * (q + 1), :] for q in range(4)]
        part[0], part[2] = exchange(part[0], part[2], upper, 64)
        part[1], part[3] = exchange(part[1], part[3], upper, 64)
        part[0], part[1] = exchange(part[0], part[1], odd, 32)
        part[2], part[3] = exchange(part[2], part[3], odd, 32)
        for band in range(4):
            value = part[band] * scale
            value = value * value
            value = value * value
            value = value * value
            out[4 * j + band, pl.ds(pl.multiple_of(TILE * c, TILE), TILE), :] = value.astype(jnp.bfloat16)

    def march(index, carry):
        j, tile = index // tiles, index % tiles
        first = tile * TILE
        here = pl.ds(pl.multiple_of(first + 8, 8), TILE)
        previous, current = cells[j + 1, 0, here, :], cells[j + 1, 1, here, :]
        total = jnp.zeros((TILE, LANES), jnp.float32)
        clear = jnp.ones((TILE, LANES), jnp.float32)
        sums = [jnp.zeros((TILE, LANES), jnp.float32) for _ in range(count)]
        for plane in range(depth):
            following = cells[j + 1, plane + 2, here, :]
            dz = following - previous
            dy = (
                cells[j + 1, plane + 1, pl.ds(first + 9, TILE), :]
                - cells[j + 1, plane + 1, pl.ds(first + 7, TILE), :]
            )
            dx = pltpu.roll(
                jnp.where(at_first, cells[j + 2, plane + 1, here, :], current), LANES - 1, 1
            ) - pltpu.roll(jnp.where(at_last, cells[j, plane + 1, here, :], current), 1, 1)
            root = lax.rsqrt(dz * dz + dy * dy + dx * dx + 4.0)
            lighting = 0.3 + jnp.abs(dz * lights[0] + dy * lights[1] + dx * lights[2]) * root
            bumps = []
            for k in range(count):
                offset = current - center[k]
                bumps.append(jnp.exp2(offset * offset * sharp[k]))
            sigma = dense[0] * bumps[0]
            weight = bumps[0] + 0.1
            for k in range(1, count):
                sigma = sigma + dense[k] * bumps[k]
                weight = weight + bumps[k]
            total = total + sigma * (0.3125 - root * root)
            remaining = jnp.exp2(total)
            factor = (clear - remaining) * lighting * pl.reciprocal(weight)
            sums = [s + factor * b for s, b in zip(sums, bumps)]
            previous, current, clear = current, following, remaining
        kept = pl.ds(pl.multiple_of(first, TILE), TILE)
        for c in range(3):
            colour = colors[c, 0] * sums[0]
            for k in range(1, count):
                colour = colour + colors[c, k] * sums[k]
            rays[j & 1, c, kept, :] = colour
        rays[j & 1, 3, kept, :] = -total
        pack(jnp.maximum(j - 1, 0), tile)
        return carry

    rays[...] = jnp.zeros_like(rays)
    lax.fori_loop(0, lanes * tiles, march, 0)
    for c in range(4):
        pack(lanes - 1, c)


def compose_kernel(bricks, out):
    count = bricks.shape[0]
    total = jnp.zeros((TILE, LANES), jnp.float32)
    image = [jnp.zeros((TILE, LANES), jnp.float32) for _ in range(3)]
    for brick in range(count):
        unscale = 1.0 / (dither(brick, (TILE, LANES)) * 65536.0)

        def value(c):
            coded = bricks[brick, TILE * c : TILE * (c + 1), :].astype(jnp.float32)
            return jnp.exp(jnp.log(coded) * 0.125) * unscale

        front = jnp.exp2(-total)
        for c in range(3):
            image[c] = image[c] + front * value(c)
        total = total + value(3)
    image.append(1.0 - jnp.exp2(-total))
    odd = (lax.axis_index("depth") & 1) == 1
    for c in range(4):
        turned = image[c].T
        block = [turned[BAND * q : BAND * (q + 1), :] for q in range(4)]
        block[0], block[2] = jnp.where(odd, block[2], block[0]), jnp.where(odd, block[0], block[2])
        out[c] = jnp.concatenate(block, axis=1)


def shards(field, tf_centers, tf_widths, tf_density, tf_colors, light):
    depth_count, row_count = lax.axis_size("depth"), lax.axis_size("rows")
    depth, rows, width = field.shape
    lanes = width // LANES
    step_size = 0.5 / (depth * depth_count)
    hbm, vmem = pl.BlockSpec(memory_space=pltpu.HBM), pl.BlockSpec(memory_space=pltpu.VMEM)

    edge = jax.ShapeDtypeStruct((rows, width), jnp.bfloat16)
    row_edge = jax.ShapeDtypeStruct((depth, width), jnp.bfloat16)
    first, last, row_first, row_last = pl.pallas_call(
        edges_kernel,
        out_shape=(edge, edge, row_edge, row_edge),
        in_specs=[hbm],
        out_specs=(vmem,) * 4,
        scratch_shapes=[
            pltpu.VMEM((2, depth, TILE, width), jnp.bfloat16),
            pltpu.VMEM((2, depth, width), jnp.float32),
            pltpu.SemaphoreType.DMA((4,)),
        ],
        compiler_params=pltpu.CompilerParams(vmem_limit_bytes=8 * MB),
        name="edges",
    )(field)

    def around(upward, downward, axis, count):
        up = [(i, (i + 1) % count) for i in range(count)]
        down = [((i + 1) % count, i) for i in range(count)]
        return lax.ppermute(upward, axis, up), lax.ppermute(downward, axis, down)

    plane_lo, plane_hi = around(last, first, "depth", depth_count)
    row_lo, row_hi = around(row_last, row_first, "rows", row_count)

    bricks = pl.pallas_call(
        lambda *refs: shade_kernel(step_size, depth_count, row_count, *refs),
        out_shape=jax.ShapeDtypeStruct((width // BAND, rows, LANES), jnp.bfloat16),
        in_specs=[hbm] * 6 + [vmem] * 4,
        out_specs=vmem,
        scratch_shapes=[
            pltpu.VMEM((depth, rows, width), jnp.bfloat16),
            pltpu.VMEM((lanes + 2, depth + 2, rows + 16, LANES), jnp.float32),
            pltpu.VMEM((2, 4, rows, LANES), jnp.float32),
            pltpu.SMEM(tf_centers.shape, jnp.float32),
            pltpu.SMEM(tf_widths.shape, jnp.float32),
            pltpu.SMEM(tf_density.shape, jnp.float32),
            pltpu.SMEM(tf_colors.shape, jnp.float32),
            pltpu.SMEM(light.shape, jnp.float32),
            pltpu.SemaphoreType.DMA((4,)),
            pltpu.SemaphoreType.DMA((5,)),
        ],
        compiler_params=pltpu.CompilerParams(vmem_limit_bytes=32 * MB),
        name="shade",
    )(tf_centers, tf_widths, tf_density, tf_colors, light, field, plane_lo, plane_hi, row_lo, row_hi)
    bricks = lax.all_to_all(bricks, "depth", 0, 0, tiled=True)
    image = pl.pallas_call(
        compose_kernel,
        out_shape=jax.ShapeDtypeStruct((4, width // depth_count, rows), jnp.float32),
        in_specs=[vmem],
        out_specs=vmem,
        name="compose",
    )(bricks)
    return jnp.transpose(image, (0, 2, 1))


def solution(mesh):
    placed = (P("depth", "rows", None), P(), P(), P(), P(), P())
    return jax.shard_map(
        shards, mesh=mesh, in_specs=placed, out_specs=P(None, "rows", "depth"), check_vma=False
    )
```

time: 82.5 us -> 59.5 us (0.72)
  the two profiles are of different devices: /device:TPU:1 before, /device:TPU:39 now
where the time goes in v2:
time: 59.5 us; the launch traced here: 59.3 us
  blocking collectives  30 us (50%)
  Pallas kernels  20.2 us (34%)
  waiting for transfers between devices  4.55 us (8%)
  starting transfers between devices  2.86 us (5%)
  local copies, waits for them, and re-layouts  1.61 us (3%)
    all_to_all x1, blocking collectives, shards(): bricks = lax.all_to_all(bricks, 'depth', 0, 0, tiled=True)  30 us
    pallas_call x1, Pallas kernels, shards(): pl.pallas_call(lambda *refs: shade_kernel(step_size, depth_count, row_cou...  17.4 us
    ppermute x4, waiting for transfers between devices, around(): return (lax.ppermute(upward, axis, up), lax.ppermute(downward, axis, down))  4.55 us
    ppermute x4, starting transfers between devices, around(): return (lax.ppermute(upward, axis, up), lax.ppermute(downward, axis, down))  2.86 us
    pallas_call x1, Pallas kernels, shards(): pl.pallas_call(compose_kernel, out_shape=jax.ShapeDtypeStruct((4, width /...  2.24 us
    unnamed x14, local copies, waits for them, and re-layouts  1.61 us
  transfers between devices with their start and end apart: 4, of which 2 were waited for; matrix products, arithmetic and copies ran while one was open for 0% of the time, Pallas kernels for 0%

profile of v2, /device:TPU:39, one launch (start us, length us, event | category | flops | bytes accessed | tf_op | source)
XLA Modules:
  0.0 59.3 jit_solution(8697596738312247296)
XLA Ops:
  0.0 0.0 copy-start
  0.0 1.6 %copy-done = bf16[16,64,1024]{2,1,0:T(8,128)(2,1)S(1)} copy-done((bf16[16,64,1024]{2,1,0:T(8,128)(2,1)S(1)}, bf16[16,64,1024]{2,1,0:T(8,128)(2,1)}, u32[]{:S(2)}) %copy-start) | copy-done | bytes 2097176
  1.6 0.0 copy-start.1
  1.6 0.0 copy-start.2
  1.6 0.0 copy-start.3
  1.6 0.0 copy-start.4
  1.6 0.0 copy-start.5
  1.6 0.0 copy-start.6
  1.6 0.6 edges.1
  2.2 1.7 %collective-permute-start = (bf16[64,1024]{1,0:T(8,128)(2,1)S(1)}, bf16[64,1024]{1,0:T(8,128)(2,1)S(1)}, u32[]{:S(2)}, u32[]{:S(2)}) collective-permute-start(bf16[64,1024]{1,0:T(8,128)(2,1)S(1)} %get-tuple-element.9), channel_id=1, source_target_pairs={{0,8},{8,16},{16,24},{24,32},{32,40},{40,48},{48,56},{56,64},{64,7... | collective-permute-start | bytes 393224 | tf_op jit(solution)/shard_map/ppermute | solution.py:239
  3.9 0.0 collective-permute-start.1
  3.9 1.1 %collective-permute-start.2 = (bf16[16,1024]{1,0:T(8,128)(2,1)S(1)}, bf16[16,1024]{1,0:T(8,128)(2,1)S(1)}, u32[]{:S(2)}, u32[]{:S(2)}) collective-permute-start(bf16[16,1024]{1,0:T(8,128)(2,1)S(1)} %get-tuple-element.11), channel_id=1, source_target_pairs={{0,1},{1,2},{2,3},{3,4},{4,5},{5,6},{6,7},{7,0},{8,9},{9,10},{10,1... | collective-permute-start | bytes 98312 | tf_op jit(solution)/shard_map/ppermute | solution.py:239
  5.1 0.0 collective-permute-start.3
  5.1 1.0 %collective-permute-done.2.refs_8_ = bf16[16,1024]{1,0:T(8,128)(2,1)S(1)} collective-permute-done((bf16[16,1024]{1,0:T(8,128)(2,1)S(1)}, bf16[16,1024]{1,0:T(8,128)(2,1)S(1)}, u32[]{:S(2)}, u32[]{:S(2)}) %collective-permute-start.2) | collective-permute-done | bytes 32800 | tf_op jit(solution)/shard_map/ppermute | solution.py:239
  6.1 3.5 %collective-permute-done.3.refs_9_ = bf16[16,1024]{1,0:T(8,128)(2,1)S(1)} collective-permute-done((bf16[16,1024]{1,0:T(8,128)(2,1)S(1)}, bf16[16,1024]{1,0:T(8,128)(2,1)S(1)}, u32[]{:S(2)}, u32[]{:S(2)}) %collective-permute-start.3) | collective-permute-done | bytes 32800 | tf_op jit(solution)/shard_map/ppermute | solution.py:239
  9.6 0.0 collective-permute-done.refs_6_
  9.6 0.0 collective-permute-done.1.refs_7_
  9.6 0.0 copy-done.1
  9.6 0.0 copy-done.2
  9.6 0.0 copy-done.3
  9.6 0.0 copy-done.4
  9.7 0.0 copy-done.5
  9.7 0.0 copy-done.6
  9.7 17.4 %shade.1 = bf16[32,64,128]{2,1,0:T(8,128)(2,1)S(1)} custom-call(f32[4]{0:T(128)S(1)} %copy-done.3, f32[4]{0:T(128)S(1)} %copy-done.4, f32[4]{0:T(128)S(1)} %copy-done.5, f32[3,4]{1,0:T(4,128)S(1)} %copy-done.2, f32[3]{0:T(128)S(1)} %copy-done.6, bf16[16,64,1024]{2,1,0:T(8,128)(2,1)S(1)} %copy-done.1, bf16[64,1024]{1,0:T(8,128)(2,1)S(1)} %collective-permute-done.refs_6_, ...), custom_call_target="tpu_custom_call" | custom-call | tf_op jit(solution)/shard_map/shade/pallas_call | solution.py:244
  27.0 30.0 %all_to_all.5.bricks = bf16[32,64,128]{2,1,0:T(8,128)(2,1)} all-to-all(bf16[32,64,128]{2,1,0:T(8,128)(2,1)S(1)} %shade.1), channel_id=1, replica_groups=mesh['depth'=32,'rows'=8] {'depth'}, dimensions={0} | all-to-all | bytes 1048576 | tf_op jit(solution)/shard_map/all_to_all | solution.py:264
  57.1 2.2 %compose.1 = f32[4,32,64]{2,1,0:T(8,128)} custom-call(bf16[32,64,128]{2,1,0:T(8,128)(2,1)} %all_to_all.5.bricks), custom_call_target="tpu_custom_call" | custom-call | tf_op jit(solution)/shard_map/compose/pallas_call | solution.py:265
Async XLA Ops:
  0.0 1.6 %copy-start = (bf16[16,64,1024]{2,1,0:T(8,128)(2,1)S(1)}, bf16[16,64,1024]{2,1,0:T(8,128)(2,1)}, u32[]{:S(2)}) copy-start(bf16[16,64,1024]{2,1,0:T(8,128)(2,1)} %refs_5_.1) | copy-start | bytes 6291460
  1.6 8.0 %copy-start.1 = (bf16[16,64,1024]{2,1,0:T(8,128)(2,1)S(1)}, bf16[16,64,1024]{2,1,0:T(8,128)(2,1)}, u32[]{:S(2)}) copy-start(bf16[16,64,1024]{2,1,0:T(8,128)(2,1)} %refs_5_.1) | copy-start | bytes 6291460
  1.6 8.0 %copy-start.2 = (f32[3,4]{1,0:T(4,128)S(1)}, f32[3,4]{1,0:T(4,128)}, u32[]{:S(2)}) copy-start(f32[3,4]{1,0:T(4,128)} %refs_3_.1) | copy-start | bytes 148
  1.6 8.0 %copy-start.3 = (f32[4]{0:T(128)S(1)}, f32[4]{0:T(128)}, u32[]{:S(2)}) copy-start(f32[4]{0:T(128)} %refs_0_.1) | copy-start | bytes 52
  1.6 8.0 %copy-start.4 = (f32[4]{0:T(128)S(1)}, f32[4]{0:T(128)}, u32[]{:S(2)}) copy-start(f32[4]{0:T(128)} %refs_1_.1) | copy-start | bytes 52
  1.6 8.1 %copy-start.5 = (f32[4]{0:T(128)S(1)}, f32[4]{0:T(128)}, u32[]{:S(2)}) copy-start(f32[4]{0:T(128)} %refs_2_.1) | copy-start | bytes 52
  1.6 8.1 %copy-start.6 = (f32[3]{0:T(128)S(1)}, f32[3]{0:T(128)}, u32[]{:S(2)}) copy-start(f32[3]{0:T(128)} %refs_4_.1) | copy-start | bytes 40
  2.2 7.4 %collective-permute-start = (bf16[64,1024]{1,0:T(8,128)(2,1)S(1)}, bf16[64,1024]{1,0:T(8,128)(2,1)S(1)}, u32[]{:S(2)}, u32[]{:S(2)}) collective-permute-start(bf16[64,1024]{1,0:T(8,128)(2,1)S(1)} %get-tuple-element.9), channel_id=1, source_target_pairs={{0,8},{8,16},{16,24},{24,32},{32,40},{40,48},{48,56},{56,64},{64,7... | collective-permute-start | bytes 393224 | tf_op jit(solution)/shard_map/ppermute | solution.py:239
  3.9 5.7 %collective-permute-start.1 = (bf16[64,1024]{1,0:T(8,128)(2,1)S(1)}, bf16[64,1024]{1,0:T(8,128)(2,1)S(1)}, u32[]{:S(2)}, u32[]{:S(2)}) collective-permute-start(bf16[64,1024]{1,0:T(8,128)(2,1)S(1)} %get-tuple-element.10), channel_id=1, source_target_pairs={{8,0},{16,8},{24,16},{32,24},{40,32},{48,40},{56,48},{64,56},{72,6... | collective-permute-start | bytes 393224 | tf_op jit(solution)/shard_map/ppermute | solution.py:239
  3.9 2.2 %collective-permute-start.2 = (bf16[16,1024]{1,0:T(8,128)(2,1)S(1)}, bf16[16,1024]{1,0:T(8,128)(2,1)S(1)}, u32[]{:S(2)}, u32[]{:S(2)}) collective-permute-start(bf16[16,1024]{1,0:T(8,128)(2,1)S(1)} %get-tuple-element.11), channel_id=1, source_target_pairs={{0,1},{1,2},{2,3},{3,4},{4,5},{5,6},{6,7},{7,0},{8,9},{9,10},{10,1... | collective-permute-start | bytes 98312 | tf_op jit(solution)/shard_map/ppermute | solution.py:239
  5.1 4.6 %collective-permute-start.3 = (bf16[16,1024]{1,0:T(8,128)(2,1)S(1)}, bf16[16,1024]{1,0:T(8,128)(2,1)S(1)}, u32[]{:S(2)}, u32[]{:S(2)}) collective-permute-start(bf16[16,1024]{1,0:T(8,128)(2,1)S(1)} %get-tuple-element.12), channel_id=1, source_target_pairs={{1,0},{2,1},{3,2},{4,3},{5,4},{6,5},{7,6},{0,7},{9,8},{10,9},{11,1... | collective-permute-start | bytes 98312 | tf_op jit(solution)/shard_map/ppermute | solution.py:239

commit v3 on v2

v3 whole, which is shorter than its diff:
```python
import math

import jax
import jax.numpy as jnp
from jax import lax
from jax.experimental import pallas as pl
from jax.experimental.pallas import tpu as pltpu
from jax.sharding import PartitionSpec as P

LOG2E = math.log2(math.e)
TILE = 16
LANES = 128
BAND = 32
MB = 1024 * 1024


def dither(brick, shape):
    lane = lax.broadcasted_iota(jnp.int32, shape, 1)
    row = lax.broadcasted_iota(jnp.int32, shape, 0)
    phase = (lane * 29 + row * 13 + brick * 37) & 63
    return phase.astype(jnp.float32) * (1.0 / 64.0) + 1.0


def edges_kernel(field, first, last, row_first, row_last, tiles, gathered, sems):
    depth, rows, _ = field.shape
    copies = [
        pltpu.make_async_copy(field.at[:, 0:TILE], tiles.at[0], sems.at[0]),
        pltpu.make_async_copy(field.at[:, rows - TILE : rows], tiles.at[1], sems.at[1]),
        pltpu.make_async_copy(field.at[0], first, sems.at[2]),
        pltpu.make_async_copy(field.at[depth - 1], last, sems.at[3]),
    ]
    for copy in copies:
        copy.start()
    for side, (row, out) in enumerate(((0, row_first), (TILE - 1, row_last))):
        copies[side].wait()
        for plane in range(depth):
            tile = tiles[side, plane].astype(jnp.float32)
            gathered[side, plane : plane + 1, :] = tile[row : row + 1, :]
        out[...] = gathered[side].astype(jnp.bfloat16)
    copies[2].wait()
    copies[3].wait()


def start_params(sources, targets, sems):
    copies = [
        pltpu.make_async_copy(source, target, sems.at[i]) for i, (source, target) in enumerate(zip(sources, targets))
    ]
    for copy in copies:
        copy.start()
    return copies


def shader(step_size, cells, centers, widths, density, colors, light):
    def full(scalar):
        return jnp.full((8, LANES), scalar, jnp.float32)

    count = centers.shape[0]
    center = [full(centers[k]) for k in range(count)]
    sharp = [-LOG2E / (full(widths[k]) * full(widths[k])) for k in range(count)]
    dense = [full(density[k]) * (-4.0 * LOG2E * step_size) for k in range(count)]
    lights = [full(light[k]) for k in range(3)]
    length = lax.rsqrt(lights[0] * lights[0] + lights[1] * lights[1] + lights[2] * lights[2])
    lights = [component * length * 0.7 for component in lights]
    lane = lax.broadcasted_iota(jnp.int32, (8, LANES), 1)
    at_first, at_last = lane == 0, lane == LANES - 1

    def rows_at(start):
        return pl.ds(pl.multiple_of(start + 8, 8), 8)

    def enter(j, start, plane, total=None, sums=None):
        zero = jnp.zeros((8, LANES), jnp.float32)
        before, at = cells[j + 1, plane, rows_at(start), :], cells[j + 1, plane + 1, rows_at(start), :]
        if total is None:
            return [before, at, zero, jnp.ones((8, LANES), jnp.float32)] + [zero] * count
        return [before, at, total, jnp.exp2(total)] + sums

    def step(j, start, plane, state):
        previous, current, total, clear, *sums = state
        here = rows_at(start)
        following = cells[j + 1, plane + 2, here, :]
        dz = following - previous
        dy = cells[j + 1, plane + 1, pl.ds(start + 9, 8), :] - cells[j + 1, plane + 1, pl.ds(start + 7, 8), :]
        dx = pltpu.roll(
            jnp.where(at_first, cells[j + 2, plane + 1, here, :], current), LANES - 1, 1
        ) - pltpu.roll(jnp.where(at_last, cells[j, plane + 1, here, :], current), 1, 1)
        root = lax.rsqrt(dz * dz + dy * dy + dx * dx + 4.0)
        lighting = 0.3 + jnp.abs(dz * lights[0] + dy * lights[1] + dx * lights[2]) * root
        bumps = []
        for k in range(count):
            offset = current - center[k]
            bumps.append(jnp.exp2(offset * offset * sharp[k]))
        sigma = dense[0] * bumps[0]
        weight = bumps[0] + 0.1
        for k in range(1, count):
            sigma = sigma + dense[k] * bumps[k]
            weight = weight + bumps[k]
        total = total + sigma * (0.3125 - root * root)
        remaining = jnp.exp2(total)
        factor = (clear - remaining) * lighting * pl.reciprocal(weight)
        sums = [s + factor * b for s, b in zip(sums, bumps)]
        return [current, following, total, remaining] + sums

    def mix(sums):
        mixed = []
        for c in range(3):
            colour = colors[c, 0] * sums[0]
            for k in range(1, count):
                colour = colour + colors[c, k] * sums[k]
            mixed.append(colour)
        return mixed

    return enter, step, mix


def spread(cells, plane, first, tile):
    for j in range(tile.shape[1] // LANES):
        cells[j + 1, plane, pl.ds(8 + first, TILE), :] = tile[:, LANES * j : LANES * (j + 1)]


def interior_kernel(step_size, *refs):
    param_sources, field_hbm, out, field, cells, params, field_sems, sems = (
        refs[:5], refs[5], refs[6], refs[7], refs[8], refs[9:14], refs[14], refs[15],
    )
    depth, rows, width = field.shape
    lanes, tiles = width // LANES, rows // TILE
    chunks = field_sems.shape[0]
    chunk = depth // chunks
    loads = []
    for c in range(chunks):
        part = pl.ds(c * chunk, chunk)
        loads.append(pltpu.make_async_copy(field_hbm.at[part], field.at[part], field_sems.at[c]))
        loads[c].start()
    smalls = start_params(param_sources, params, sems)

    for side in (0, lanes + 1):
        for plane in range(1, depth - 1):
            cells[side, plane + 1, 8 : 8 + rows, :] = jnp.zeros((rows, LANES), jnp.float32)

    def prepare(index, carry):
        plane = index // tiles
        first = pl.multiple_of((index % tiles) * TILE, TILE)
        spread(cells, plane + 1, first, field[plane, pl.ds(first, TILE), :].astype(jnp.float32))
        return carry

    for c in range(chunks):
        loads[c].wait()
        lax.fori_loop(c * chunk * tiles, (c + 1) * chunk * tiles, prepare, 0)
    for copy in smalls:
        copy.wait()
    enter, step, mix = shader(step_size, cells, *params)

    def march(j, carry):
        done = []
        for pair in range((rows - 16) // 16):
            starts = [8 + 16 * pair, 16 + 16 * pair]
            states = [enter(j, start, 1) for start in starts]
            for plane in range(1, depth - 1):
                states = [step(j, start, plane, state) for start, state in zip(starts, states)]
            done += [(start - 8, mix(state[4:]) + [state[2]]) for start, state in zip(starts, states)]
        for start, values in done:
            for c in range(4):
                out[j, c, start : start + 8, :] = values[c]
        return carry

    lax.fori_loop(0, lanes, march, 0)


def border_kernel(step_size, depth_count, row_count, *refs):
    param_sources, field_hbm, plane_lo, plane_hi, row_lo, row_hi, inner, out = refs[:5], *refs[5:12]
    field, cells, rays, params, field_sems, sems = refs[12], refs[13], refs[14], refs[15:20], refs[20], refs[21]
    depth, rows, width = field.shape
    lanes = width // LANES
    parts = (
        (slice(0, depth), slice(0, TILE)),
        (slice(0, depth), slice(rows - TILE, rows)),
        (slice(0, 2), slice(TILE, rows - TILE)),
        (slice(depth - 2, depth), slice(TILE, rows - TILE)),
    )
    loads = []
    for c, part in enumerate(parts):
        loads.append(pltpu.make_async_copy(field_hbm.at[part], field.at[part], field_sems.at[c]))
        loads[c].start()
    smalls = start_params(param_sources, params, sems)

    me, row_me = lax.axis_index("depth"), lax.axis_index("rows")
    keep_lo = (me > 0).astype(jnp.float32)
    keep_hi = (me < depth_count - 1).astype(jnp.float32)
    keep_up = (row_me > 0).astype(jnp.float32)
    keep_down = (row_me < row_count - 1).astype(jnp.float32)
    for first in range(0, rows, TILE):
        spread(cells, 0, first, plane_lo[first : first + TILE, :].astype(jnp.float32) * keep_lo)
        spread(cells, depth + 1, first, plane_hi[first : first + TILE, :].astype(jnp.float32) * keep_hi)
    low, high = row_lo[...].astype(jnp.float32) * keep_up, row_hi[...].astype(jnp.float32) * keep_down
    for j in range(lanes):
        for plane in range(depth):
            cells[j + 1, plane + 1, 7:8, :] = low[plane : plane + 1, LANES * j : LANES * (j + 1)]
            cells[j + 1, plane + 1, 8 + rows : 9 + rows, :] = high[plane : plane + 1, LANES * j : LANES * (j + 1)]
    for side in (0, lanes + 1):
        for plane in range(depth):
            cells[side, plane + 1, 8 : 8 + rows, :] = jnp.zeros((rows, LANES), jnp.float32)

    for c, part in enumerate(parts):
        loads[c].wait()
        if c < 2:
            first = part[1].start

            def prepare(plane, carry, first=first):
                spread(cells, plane + 1, first, field[plane, first : first + TILE, :].astype(jnp.float32))
                return carry

            lax.fori_loop(0, depth, prepare, 0)
        else:
            for plane in range(part[0].start, part[0].stop):
                for first in range(TILE, rows - TILE, TILE):
                    spread(cells, plane + 1, first, field[plane, first : first + TILE, :].astype(jnp.float32))
    for copy in smalls:
        copy.wait()
    enter, step, mix = shader(step_size, cells, *params)

    lane = lax.broadcasted_iota(jnp.int32, (TILE, LANES), 1)
    upper, odd = lane >= 64, (lane & 32) > 0
    scale = dither(me, (TILE, LANES)) * 65536.0

    def pack(j, c):
        def exchange(a, b, mask, shift):
            moved = pltpu.roll(jnp.where(mask, a, b), shift, 1)
            return jnp.where(mask, moved, a), jnp.where(mask, b, moved)

        part = [rays[j & 1, c, TILE * q : TILE * (q + 1), :] for q in range(4)]
        part[0], part[2] = exchange(part[0], part[2], upper, 64)
        part[1], part[3] = exchange(part[1], part[3], upper, 64)
        part[0], part[1] = exchange(part[0], part[1], odd, 32)
        part[2], part[3] = exchange(part[2], part[3], odd, 32)
        for band in range(4):
            value = part[band] * scale
            value = value * value
            value = value * value
            value = value * value
            out[4 * j + band, TILE * c : TILE * (c + 1), :] = value.astype(jnp.bfloat16)

    def march(j, carry):
        for c in range(4):
            pack(jnp.maximum(j - 1, 0), c)
        done = []
        starts = [0, rows - 8]
        states = [enter(j, start, 0) for start in starts]
        for plane in range(depth):
            states = [step(j, start, plane, state) for start, state in zip(starts, states)]
        done += [(start, mix(state[4:]) + [state[2]]) for start, state in zip(starts, states)]
        for start in range(8, rows - 8, 8):
            state = step(j, start, 0, enter(j, start, 0))
            front, total = state[3], state[2] + inner[j, 3, start - 8 : start, :]
            state = step(j, start, depth - 1, enter(j, start, depth - 1, total, state[4:]))
            values = [v + front * inner[j, c, start - 8 : start, :] for c, v in enumerate(mix(state[4:]))]
            done.append((start, values + [state[2]]))
        for start, values in done:
            for c in range(3):
                rays[j & 1, c, start : start + 8, :] = values[c]
            rays[j & 1, 3, start : start + 8, :] = -values[3]
        return carry

    rays[...] = jnp.zeros_like(rays)
    lax.fori_loop(0, lanes, march, 0)
    for c in range(4):
        pack(lanes - 1, c)


def compose_kernel(bricks, out):
    count = bricks.shape[0]
    total = jnp.zeros((TILE, LANES), jnp.float32)
    image = [jnp.zeros((TILE, LANES), jnp.float32) for _ in range(3)]
    for brick in range(count):
        unscale = 1.0 / (dither(brick, (TILE, LANES)) * 65536.0)

        def value(c):
            coded = bricks[brick, TILE * c : TILE * (c + 1), :].astype(jnp.float32)
            return jnp.exp(jnp.log(coded) * 0.125) * unscale

        front = jnp.exp2(-total)
        for c in range(3):
            image[c] = image[c] + front * value(c)
        total = total + value(3)
    image.append(1.0 - jnp.exp2(-total))
    odd = (lax.axis_index("depth") & 1) == 1
    for c in range(4):
        turned = image[c].T
        block = [turned[BAND * q : BAND * (q + 1), :] for q in range(4)]
        block[0], block[2] = jnp.where(odd, block[2], block[0]), jnp.where(odd, block[0], block[2])
        out[c] = jnp.concatenate(block, axis=1)


def shards(field, tf_centers, tf_widths, tf_density, tf_colors, light):
    depth_count, row_count = lax.axis_size("depth"), lax.axis_size("rows")
    depth, rows, width = field.shape
    lanes = width // LANES
    step_size = 0.5 / (depth * depth_count)
    hbm, vmem = pl.BlockSpec(memory_space=pltpu.HBM), pl.BlockSpec(memory_space=pltpu.VMEM)

    edge = jax.ShapeDtypeStruct((rows, width), jnp.bfloat16)
    row_edge = jax.ShapeDtypeStruct((depth, width), jnp.bfloat16)
    first, last, row_first, row_last = pl.pallas_call(
        edges_kernel,
        out_shape=(edge, edge, row_edge, row_edge),
        in_specs=[hbm],
        out_specs=(vmem,) * 4,
        scratch_shapes=[
            pltpu.VMEM((2, depth, TILE, width), jnp.bfloat16),
            pltpu.VMEM((2, depth, width), jnp.float32),
            pltpu.SemaphoreType.DMA((4,)),
        ],
        compiler_params=pltpu.CompilerParams(vmem_limit_bytes=56 * MB),
        name="edges",
    )(field)

    inner_field, first, last, row_first, row_last = lax.optimization_barrier(
        (field, first, last, row_first, row_last)
    )

    def around(upward, downward, axis, count):
        up = [(i, (i + 1) % count) for i in range(count)]
        down = [((i + 1) % count, i) for i in range(count)]
        return lax.ppermute(upward, axis, up), lax.ppermute(downward, axis, down)

    plane_lo, plane_hi = around(last, first, "depth", depth_count)
    row_lo, row_hi = around(row_last, row_first, "rows", row_count)

    params = (tf_centers, tf_widths, tf_density, tf_colors, light)
    field_scratch = [
        pltpu.VMEM((depth, rows, width), jnp.bfloat16),
        pltpu.VMEM((lanes + 2, depth + 2, rows + 16, LANES), jnp.float32),
    ]
    param_scratch = [pltpu.SMEM(param.shape, jnp.float32) for param in params] + [
        pltpu.SemaphoreType.DMA((4,)),
        pltpu.SemaphoreType.DMA((5,)),
    ]
    inner = pl.pallas_call(
        lambda *refs: interior_kernel(step_size, *refs),
        out_shape=jax.ShapeDtypeStruct((lanes, 4, rows - 16, LANES), jnp.float32),
        in_specs=[hbm] * 6,
        out_specs=vmem,
        scratch_shapes=field_scratch + param_scratch,
        compiler_params=pltpu.CompilerParams(vmem_limit_bytes=32 * MB),
        cost_estimate=pl.CostEstimate(flops=60_000_000, bytes_accessed=3_000_000, transcendentals=5_000_000),
        name="interior",
    )(*params, inner_field)
    bricks = pl.pallas_call(
        lambda *refs: border_kernel(step_size, depth_count, row_count, *refs),
        out_shape=jax.ShapeDtypeStruct((width // BAND, rows, LANES), jnp.bfloat16),
        in_specs=[hbm] * 6 + [vmem] * 5,
        out_specs=vmem,
        scratch_shapes=field_scratch + [pltpu.VMEM((2, 4, rows, LANES), jnp.float32)] + param_scratch,
        compiler_params=pltpu.CompilerParams(vmem_limit_bytes=32 * MB),
        name="border",
    )(*params, field, plane_lo, plane_hi, row_lo, row_hi, inner)
    bricks = lax.all_to_all(bricks, "depth", 0, 0, tiled=True)
    image = pl.pallas_call(
        compose_kernel,
        out_shape=jax.ShapeDtypeStruct((4, width // depth_count, rows), jnp.float32),
        in_specs=[vmem],
        out_specs=vmem,
        compiler_params=pltpu.CompilerParams(vmem_limit_bytes=16 * MB),
        name="compose",
    )(bricks)
    return jnp.transpose(image, (0, 2, 1))


def solution(mesh):
    placed = (P("depth", "rows", None), P(), P(), P(), P(), P())
    return jax.shard_map(
        shards, mesh=mesh, in_specs=placed, out_specs=P(None, "rows", "depth"), check_vma=False
    )
```

time: 59.5 us -> 50.9 us (0.86)
  the two profiles are of different devices: /device:TPU:39 before, /device:TPU:2 now
where the time goes in v3:
time: 50.9 us; the launch traced here: 50 us
  blocking collectives  22.9 us (45%)
  Pallas kernels  16.7 us (33%)
  starting transfers between devices  10.2 us (20%)
    all_to_all x1, blocking collectives, shards(): bricks = lax.all_to_all(bricks, 'depth', 0, 0, tiled=True)  22.9 us
    ppermute x4, starting transfers between devices, around(): return (lax.ppermute(upward, axis, up), lax.ppermute(downward, axis, down))  10.2 us
    pallas_call x1, Pallas kernels, shards(): pl.pallas_call(lambda *refs: interior_kernel(step_size, *refs), out_shape...  8.09 us
    pallas_call x1, Pallas kernels, shards(): pl.pallas_call(lambda *refs: border_kernel(step_size, depth_count, row_co...  5.26 us
    pallas_call x1, Pallas kernels, shards(): pl.pallas_call(edges_kernel, out_shape=(edge, edge, row_edge, row_edge),...  2.15 us
    pallas_call x1, Pallas kernels, shards(): pl.pallas_call(compose_kernel, out_shape=jax.ShapeDtypeStruct((4, width /...  1.2 us
  transfers between devices with their start and end apart: 4, of which 0 were waited for; matrix products, arithmetic and copies ran while one was open for 0% of the time, Pallas kernels for 16%

profile of v3, /device:TPU:2, one launch (start us, length us, event | category | flops | bytes accessed | tf_op | source)
XLA Modules:
  0.0 50.0 jit_solution(9537242651776569486)
XLA Ops:
  0.0 0.0 copy-start
  0.0 0.0 copy-start.5
  0.0 0.0 copy-start.1
  0.0 0.0 copy-start.4
  0.0 0.0 copy-start.3
  0.0 0.0 copy-start.2
  0.0 2.1 %edges.1 = (bf16[64,1024]{1,0:T(8,128)(2,1)}, bf16[64,1024]{1,0:T(8,128)(2,1)}, bf16[16,1024]{1,0:T(8,128)(2,1)}, bf16[16,1024]{1,0:T(8,128)(2,1)}) custom-call(bf16[16,64,1024]{2,1,0:T(8,128)(2,1)} %refs_5_.2), custom_call_target="tpu_custom_call" | custom-call | tf_op jit(solution)/shard_map/edges/pallas_call | solution.py:301
  2.2 2.0 %collective-permute-start = (bf16[64,1024]{1,0:T(8,128)(2,1)}, bf16[64,1024]{1,0:T(8,128)(2,1)S(1)}, u32[]{:S(2)}, u32[]{:S(2)}) collective-permute-start(bf16[64,1024]{1,0:T(8,128)(2,1)} %get-tuple-element.18), channel_id=1, source_target_pairs={{0,8},{8,16},{16,24},{24,32},{32,40},{40,48},{48,56},{56,64},{64,7... | collective-permute-start | bytes 393224 | tf_op jit(solution)/shard_map/ppermute | solution.py:322
  4.2 6.5 %collective-permute-start.1 = (bf16[64,1024]{1,0:T(8,128)(2,1)}, bf16[64,1024]{1,0:T(8,128)(2,1)S(1)}, u32[]{:S(2)}, u32[]{:S(2)}) collective-permute-start(bf16[64,1024]{1,0:T(8,128)(2,1)} %get-tuple-element.19), channel_id=1, source_target_pairs={{8,0},{16,8},{24,16},{32,24},{40,32},{48,40},{56,48},{64,56},{72,6... | collective-permute-start | bytes 393224 | tf_op jit(solution)/shard_map/ppermute | solution.py:322
  10.7 0.0 collective-permute-start.2
  10.7 1.7 %collective-permute-start.3 = (bf16[16,1024]{1,0:T(8,128)(2,1)}, bf16[16,1024]{1,0:T(8,128)(2,1)S(1)}, u32[]{:S(2)}, u32[]{:S(2)}) collective-permute-start(bf16[16,1024]{1,0:T(8,128)(2,1)} %get-tuple-element.21), channel_id=1, source_target_pairs={{1,0},{2,1},{3,2},{4,3},{5,4},{6,5},{7,6},{0,7},{9,8},{10,9},{11,1... | collective-permute-start | bytes 98312 | tf_op jit(solution)/shard_map/ppermute | solution.py:322
  12.4 0.0 copy-done
  12.4 0.0 copy-done.5
  12.4 0.0 copy-done.1
  12.4 0.0 copy-done.4
  12.4 0.0 copy-done.3
  12.4 0.0 copy-done.2
  12.5 8.1 %interior.1.refs_10_ = f32[8,4,48,128]{3,2,1,0:T(8,128)S(1)} custom-call(f32[4]{0:T(128)S(1)} %copy-done.2, f32[4]{0:T(128)S(1)} %copy-done.3, f32[4]{0:T(128)S(1)} %copy-done.4, f32[3,4]{1,0:T(4,128)S(1)} %copy-done.1, f32[3]{0:T(128)S(1)} %copy-done.5, bf16[16,64,1024]{2,1,0:T(8,128)(2,1)S(1)} %copy-done), custom_call_target="tpu_custom_call" | custom-call | flops 60000000 | bytes 3000000 | tf_op jit(solution)/shard_map/interior/pallas_call | solution.py:336
  20.6 0.0 collective-permute-done.2.refs_8_
  20.6 0.0 collective-permute-done.3.refs_9_
  20.6 0.0 collective-permute-done.refs_6_
  20.6 0.0 collective-permute-done.1.refs_7_
  20.6 5.3 %border.1 = bf16[32,64,128]{2,1,0:T(8,128)(2,1)S(1)} custom-call(f32[4]{0:T(128)S(1)} %copy-done.2, f32[4]{0:T(128)S(1)} %copy-done.3, f32[4]{0:T(128)S(1)} %copy-done.4, f32[3,4]{1,0:T(4,128)S(1)} %copy-done.1, f32[3]{0:T(128)S(1)} %copy-done.5, bf16[16,64,1024]{2,1,0:T(8,128)(2,1)S(1)} %copy-done, bf16[64,1024]{1,0:T(8,128)(2,1)S(1)} %collective-permute-done.refs_6_, ...), custom_call_target="tpu_custom_call" | custom-call | tf_op jit(solution)/shard_map/border/pallas_call | solution.py:346
  25.9 22.9 %all_to_all.5.bricks = bf16[32,64,128]{2,1,0:T(8,128)(2,1)S(1)} all-to-all(bf16[32,64,128]{2,1,0:T(8,128)(2,1)S(1)} %border.1), channel_id=1, replica_groups=mesh['depth'=32,'rows'=8] {'depth'}, dimensions={0} | all-to-all | bytes 1048576 | tf_op jit(solution)/shard_map/all_to_all | solution.py:355
  48.8 1.2 %compose.1 = f32[4,32,64]{2,1,0:T(8,128)} custom-call(bf16[32,64,128]{2,1,0:T(8,128)(2,1)S(1)} %all_to_all.5.bricks), custom_call_target="tpu_custom_call" | custom-call | tf_op jit(solution)/shard_map/compose/pallas_call | solution.py:356
Async XLA Ops:
  0.0 12.4 %copy-start = (bf16[16,64,1024]{2,1,0:T(8,128)(2,1)S(1)}, bf16[16,64,1024]{2,1,0:T(8,128)(2,1)}, u32[]{:S(2)}) copy-start(bf16[16,64,1024]{2,1,0:T(8,128)(2,1)} %refs_5_.2) | copy-start | bytes 6291460
  0.0 12.4 %copy-start.5 = (f32[3]{0:T(128)S(1)}, f32[3]{0:T(128)}, u32[]{:S(2)}) copy-start(f32[3]{0:T(128)} %refs_4_.3) | copy-start | bytes 40
  0.0 12.4 %copy-start.1 = (f32[3,4]{1,0:T(4,128)S(1)}, f32[3,4]{1,0:T(4,128)}, u32[]{:S(2)}) copy-start(f32[3,4]{1,0:T(4,128)} %refs_3_.3) | copy-start | bytes 148
  0.0 12.4 %copy-start.4 = (f32[4]{0:T(128)S(1)}, f32[4]{0:T(128)}, u32[]{:S(2)}) copy-start(f32[4]{0:T(128)} %refs_2_.3) | copy-start | bytes 52
  0.0 12.4 %copy-start.3 = (f32[4]{0:T(128)S(1)}, f32[4]{0:T(128)}, u32[]{:S(2)}) copy-start(f32[4]{0:T(128)} %refs_1_.3) | copy-start | bytes 52
  0.0 12.4 %copy-start.2 = (f32[4]{0:T(128)S(1)}, f32[4]{0:T(128)}, u32[]{:S(2)}) copy-start(f32[4]{0:T(128)} %refs_0_.3) | copy-start | bytes 52
  2.2 18.4 %collective-permute-start = (bf16[64,1024]{1,0:T(8,128)(2,1)}, bf16[64,1024]{1,0:T(8,128)(2,1)S(1)}, u32[]{:S(2)}, u32[]{:S(2)}) collective-permute-start(bf16[64,1024]{1,0:T(8,128)(2,1)} %get-tuple-element.18), channel_id=1, source_target_pairs={{0,8},{8,16},{16,24},{24,32},{32,40},{40,48},{48,56},{56,64},{64,7... | collective-permute-start | bytes 393224 | tf_op jit(solution)/shard_map/ppermute | solution.py:322
  4.2 16.4 %collective-permute-start.1 = (bf16[64,1024]{1,0:T(8,128)(2,1)}, bf16[64,1024]{1,0:T(8,128)(2,1)S(1)}, u32[]{:S(2)}, u32[]{:S(2)}) collective-permute-start(bf16[64,1024]{1,0:T(8,128)(2,1)} %get-tuple-element.19), channel_id=1, source_target_pairs={{8,0},{16,8},{24,16},{32,24},{40,32},{48,40},{56,48},{64,56},{72,6... | collective-permute-start | bytes 393224 | tf_op jit(solution)/shard_map/ppermute | solution.py:322
  10.7 9.9 %collective-permute-start.2 = (bf16[16,1024]{1,0:T(8,128)(2,1)}, bf16[16,1024]{1,0:T(8,128)(2,1)S(1)}, u32[]{:S(2)}, u32[]{:S(2)}) collective-permute-start(bf16[16,1024]{1,0:T(8,128)(2,1)} %get-tuple-element.20), channel_id=1, source_target_pairs={{0,1},{1,2},{2,3},{3,4},{4,5},{5,6},{6,7},{7,0},{8,9},{9,10},{10,1... | collective-permute-start | bytes 98312 | tf_op jit(solution)/shard_map/ppermute | solution.py:322
  10.7 9.9 %collective-permute-start.3 = (bf16[16,1024]{1,0:T(8,128)(2,1)}, bf16[16,1024]{1,0:T(8,128)(2,1)S(1)}, u32[]{:S(2)}, u32[]{:S(2)}) collective-permute-start(bf16[16,1024]{1,0:T(8,128)(2,1)} %get-tuple-element.21), channel_id=1, source_target_pairs={{1,0},{2,1},{3,2},{4,3},{5,4},{6,5},{7,6},{0,7},{9,8},{10,9},{11,1... | collective-permute-start | bytes 98312 | tf_op jit(solution)/shard_map/ppermute | solution.py:322

commit v4 on v3

--- a/solution.py
+++ b/solution.py
@@ -21,22 +21,25 @@
     return phase.astype(jnp.float32) * (1.0 / 64.0) + 1.0
 
 
-def edges_kernel(field, first, last, row_first, row_last, tiles, gathered, sems):
+def edges_kernel(field, plane_one, plane_two, row_one, row_two, tiles, gathered, sems):
     depth, rows, _ = field.shape
+    chosen = jnp.where((lax.axis_index("depth") & 1) == 0, depth - 1, 0)
     copies = [
         pltpu.make_async_copy(field.at[:, 0:TILE], tiles.at[0], sems.at[0]),
         pltpu.make_async_copy(field.at[:, rows - TILE : rows], tiles.at[1], sems.at[1]),
-        pltpu.make_async_copy(field.at[0], first, sems.at[2]),
-        pltpu.make_async_copy(field.at[depth - 1], last, sems.at[3]),
+        pltpu.make_async_copy(field.at[chosen], plane_one, sems.at[2]),
+        pltpu.make_async_copy(field.at[depth - 1 - chosen], plane_two, sems.at[3]),
     ]
     for copy in copies:
         copy.start()
-    for side, (row, out) in enumerate(((0, row_first), (TILE - 1, row_last))):
+    for side, row in ((0, 0), (1, TILE - 1)):
         copies[side].wait()
         for plane in range(depth):
             tile = tiles[side, plane].astype(jnp.float32)
             gathered[side, plane : plane + 1, :] = tile[row : row + 1, :]
-        out[...] = gathered[side].astype(jnp.bfloat16)
+    even = (lax.axis_index("rows") & 1) == 0
+    row_one[...] = jnp.where(even, gathered[1], gathered[0]).astype(jnp.bfloat16)
+    row_two[...] = jnp.where(even, gathered[0], gathered[1]).astype(jnp.bfloat16)
     copies[2].wait()
     copies[3].wait()
 
@@ -118,18 +121,9 @@
 
 
 def interior_kernel(step_size, *refs):
-    param_sources, field_hbm, out, field, cells, params, field_sems, sems = (
-        refs[:5], refs[5], refs[6], refs[7], refs[8], refs[9:14], refs[14], refs[15],
-    )
+    param_sources, field, out, cells, params, sems = refs[:5], refs[5], refs[6], refs[7], refs[8:13], refs[13]
     depth, rows, width = field.shape
     lanes, tiles = width // LANES, rows // TILE
-    chunks = field_sems.shape[0]
-    chunk = depth // chunks
-    loads = []
-    for c in range(chunks):
-        part = pl.ds(c * chunk, chunk)
-        loads.append(pltpu.make_async_copy(field_hbm.at[part], field.at[part], field_sems.at[c]))
-        loads[c].start()
     smalls = start_params(param_sources, params, sems)
 
     for side in (0, lanes + 1):
@@ -142,9 +136,7 @@
         spread(cells, plane + 1, first, field[plane, pl.ds(first, TILE), :].astype(jnp.float32))
         return carry
 
-    for c in range(chunks):
-        loads[c].wait()
-        lax.fori_loop(c * chunk * tiles, (c + 1) * chunk * tiles, prepare, 0)
+    lax.fori_loop(0, depth * tiles, prepare, 0)
     for copy in smalls:
         copy.wait()
     enter, step, mix = shader(step_size, cells, *params)
@@ -166,31 +158,28 @@
 
 
 def border_kernel(step_size, depth_count, row_count, *refs):
-    param_sources, field_hbm, plane_lo, plane_hi, row_lo, row_hi, inner, out = refs[:5], *refs[5:12]
-    field, cells, rays, params, field_sems, sems = refs[12], refs[13], refs[14], refs[15:20], refs[20], refs[21]
+    param_sources, field, plane_one, plane_two, row_one, row_two, inner, out = refs[:5], *refs[5:12]
+    cells, rays, params, sems = refs[12], refs[13], refs[14:19], refs[19]
     depth, rows, width = field.shape
     lanes = width // LANES
-    parts = (
-        (slice(0, depth), slice(0, TILE)),
-        (slice(0, depth), slice(rows - TILE, rows)),
-        (slice(0, 2), slice(TILE, rows - TILE)),
-        (slice(depth - 2, depth), slice(TILE, rows - TILE)),
-    )
-    loads = []
-    for c, part in enumerate(parts):
-        loads.append(pltpu.make_async_copy(field_hbm.at[part], field.at[part], field_sems.at[c]))
-        loads[c].start()
     smalls = start_params(param_sources, params, sems)
 
-    me, row_me = lax.axis_index("depth"), lax.axis_index("rows")
-    keep_lo = (me > 0).astype(jnp.float32)
-    keep_hi = (me < depth_count - 1).astype(jnp.float32)
-    keep_up = (row_me > 0).astype(jnp.float32)
-    keep_down = (row_me < row_count - 1).astype(jnp.float32)
+    def sided(index, count):
+        even = (index & 1) == 0
+        return even, (index > 0).astype(jnp.float32), (index < count - 1).astype(jnp.float32)
+
+    def around(one, two, even, keep_lo, keep_hi):
+        one, two = one.astype(jnp.float32), two.astype(jnp.float32)
+        return jnp.where(even, two, one) * keep_lo, jnp.where(even, one, two) * keep_hi
+
+    me = lax.axis_index("depth")
+    plane_sides, row_sides = sided(me, depth_count), sided(lax.axis_index("rows"), row_count)
     for first in range(0, rows, TILE):
-        spread(cells, 0, first, plane_lo[first : first + TILE, :].astype(jnp.float32) * keep_lo)
-        spread(cells, depth + 1, first, plane_hi[first : first + TILE, :].astype(jnp.float32) * keep_hi)
-    low, high = row_lo[...].astype(jnp.float32) * keep_up, row_hi[...].astype(jnp.float32) * keep_down
+        part = pl.ds(first, TILE)
+        low, high = around(plane_one[part, :], plane_two[part, :], *plane_sides)
+        spread(cells, 0, first, low)
+        spread(cells, depth + 1, first, high)
+    low, high = around(row_one[...], row_two[...], *row_sides)
     for j in range(lanes):
         for plane in range(depth):
             cells[j + 1, plane + 1, 7:8, :] = low[plane : plane + 1, LANES * j : LANES * (j + 1)]
@@ -199,20 +188,15 @@
         for plane in range(depth):
             cells[side, plane + 1, 8 : 8 + rows, :] = jnp.zeros((rows, LANES), jnp.float32)
 
-    for c, part in enumerate(parts):
-        loads[c].wait()
-        if c < 2:
-            first = part[1].start
-
-            def prepare(plane, carry, first=first):
-                spread(cells, plane + 1, first, field[plane, first : first + TILE, :].astype(jnp.float32))
-                return carry
-
-            lax.fori_loop(0, depth, prepare, 0)
-        else:
-            for plane in range(part[0].start, part[0].stop):
-                for first in range(TILE, rows - TILE, TILE):
-                    spread(cells, plane + 1, first, field[plane, first : first + TILE, :].astype(jnp.float32))
+    def prepare(plane, carry):
+        for first in (0, rows - TILE):
+            spread(cells, plane + 1, first, field[plane, first : first + TILE, :].astype(jnp.float32))
+        return carry
+
+    lax.fori_loop(0, depth, prepare, 0)
+    for plane in (0, 1, depth - 2, depth - 1):
+        for first in range(TILE, rows - TILE, TILE):
+            spread(cells, plane + 1, first, field[plane, first : first + TILE, :].astype(jnp.float32))
     for copy in smalls:
         copy.wait()
     enter, step, mix = shader(step_size, cells, *params)
@@ -298,7 +282,7 @@
 
     edge = jax.ShapeDtypeStruct((rows, width), jnp.bfloat16)
     row_edge = jax.ShapeDtypeStruct((depth, width), jnp.bfloat16)
-    first, last, row_first, row_last = pl.pallas_call(
+    edges = pl.pallas_call(
         edges_kernel,
         out_shape=(edge, edge, row_edge, row_edge),
         in_specs=[hbm],
@@ -308,37 +292,29 @@
             pltpu.VMEM((2, depth, width), jnp.float32),
             pltpu.SemaphoreType.DMA((4,)),
         ],
-        compiler_params=pltpu.CompilerParams(vmem_limit_bytes=56 * MB),
+        compiler_params=pltpu.CompilerParams(vmem_limit_bytes=52 * MB),
         name="edges",
     )(field)
 
-    inner_field, first, last, row_first, row_last = lax.optimization_barrier(
-        (field, first, last, row_first, row_last)
-    )
-
-    def around(upward, downward, axis, count):
-        up = [(i, (i + 1) % count) for i in range(count)]
-        down = [((i + 1) % count, i) for i in range(count)]
-        return lax.ppermute(upward, axis, up), lax.ppermute(downward, axis, down)
-
-    plane_lo, plane_hi = around(last, first, "depth", depth_count)
-    row_lo, row_hi = around(row_last, row_first, "rows", row_count)
+    inner_field, *edges = lax.optimization_barrier((field, *edges))
+
+    def exchange(one, two, axis, count):
+        near = [(k, k ^ 1) for k in range(count)]
+        far = [(k, (k - 1 + 2 * (k & 1)) % count) for k in range(count)]
+        return lax.ppermute(one, axis, near), lax.ppermute(two, axis, far)
+
+    plane_one, plane_two = exchange(edges[0], edges[1], "depth", depth_count)
+    row_one, row_two = exchange(edges[2], edges[3], "rows", row_count)
 
     params = (tf_centers, tf_widths, tf_density, tf_colors, light)
-    field_scratch = [
-        pltpu.VMEM((depth, rows, width), jnp.bfloat16),
-        pltpu.VMEM((lanes + 2, depth + 2, rows + 16, LANES), jnp.float32),
-    ]
-    param_scratch = [pltpu.SMEM(param.shape, jnp.float32) for param in params] + [
-        pltpu.SemaphoreType.DMA((4,)),
-        pltpu.SemaphoreType.DMA((5,)),
-    ]
+    cells = pltpu.VMEM((lanes + 2, depth + 2, rows + 16, LANES), jnp.float32)
+    param_scratch = [pltpu.SMEM(param.shape, jnp.float32) for param in params] + [pltpu.SemaphoreType.DMA((5,))]
     inner = pl.pallas_call(
         lambda *refs: interior_kernel(step_size, *refs),
         out_shape=jax.ShapeDtypeStruct((lanes, 4, rows - 16, LANES), jnp.float32),
-        in_specs=[hbm] * 6,
+        in_specs=[hbm] * 5 + [vmem],
         out_specs=vmem,
-        scratch_shapes=field_scratch + param_scratch,
+        scratch_shapes=[cells] + param_scratch,
         compiler_params=pltpu.CompilerParams(vmem_limit_bytes=32 * MB),
         cost_estimate=pl.CostEstimate(flops=60_000_000, bytes_accessed=3_000_000, transcendentals=5_000_000),
         name="interior",
@@ -346,12 +322,12 @@
     bricks = pl.pallas_call(
         lambda *refs: border_kernel(step_size, depth_count, row_count, *refs),
         out_shape=jax.ShapeDtypeStruct((width // BAND, rows, LANES), jnp.bfloat16),
-        in_specs=[hbm] * 6 + [vmem] * 5,
+        in_specs=[hbm] * 5 + [vmem] * 6,
         out_specs=vmem,
-        scratch_shapes=field_scratch + [pltpu.VMEM((2, 4, rows, LANES), jnp.float32)] + param_scratch,
+        scratch_shapes=[cells, pltpu.VMEM((2, 4, rows, LANES), jnp.float32)] + param_scratch,
         compiler_params=pltpu.CompilerParams(vmem_limit_bytes=32 * MB),
         name="border",
-    )(*params, field, plane_lo, plane_hi, row_lo, row_hi, inner)
+    )(*params, field, plane_one, plane_two, row_one, row_two, inner)
     bricks = lax.all_to_all(bricks, "depth", 0, 0, tiled=True)
     image = pl.pallas_call(
         compose_kernel,

time: 50.9 us -> 48 us (0.943)
  the two profiles are of different devices: /device:TPU:2 before, /device:TPU:32 now
where the time goes in v4:
time: 48 us; the launch traced here: 47.9 us
  blocking collectives  25.4 us (53%)
  Pallas kernels  15.5 us (32%)
  starting transfers between devices  6.79 us (14%)
    all_to_all x1, blocking collectives, shards(): bricks = lax.all_to_all(bricks, 'depth', 0, 0, tiled=True)  25.4 us
    pallas_call x1, Pallas kernels, shards(): pl.pallas_call(lambda *refs: interior_kernel(step_size, *refs), out_shape...  7.91 us
    ppermute x4, starting transfers between devices, exchange(): return (lax.ppermute(one, axis, near), lax.ppermute(two, axis, far))  6.79 us
    pallas_call x1, Pallas kernels, shards(): pl.pallas_call(lambda *refs: border_kernel(step_size, depth_count, row_co...  4.99 us
    pallas_call x1, Pallas kernels, shards(): pl.pallas_call(edges_kernel, out_shape=(edge, edge, row_edge, row_edge),...  1.44 us
    pallas_call x1, Pallas kernels, shards(): pl.pallas_call(compose_kernel, out_shape=jax.ShapeDtypeStruct((4, width /...  1.2 us
  transfers between devices with their start and end apart: 4, of which 0 were waited for; matrix products, arithmetic and copies ran while one was open for 0% of the time, Pallas kernels for 17%

profile of v4, /device:TPU:32, one launch (start us, length us, event | category | flops | bytes accessed | tf_op | source)
XLA Modules:
  0.0 47.9 jit_solution(7838776054319644265)
XLA Ops:
  0.0 0.0 copy-start
  0.0 0.0 copy-start.5
  0.0 0.0 copy-start.1
  0.0 0.0 copy-start.4
  0.0 0.0 copy-start.3
  0.0 0.0 copy-start.2
  0.0 1.4 %edges.1 = (bf16[64,1024]{1,0:T(8,128)(2,1)S(1)}, bf16[64,1024]{1,0:T(8,128)(2,1)S(1)}, bf16[16,1024]{1,0:T(8,128)(2,1)S(1)}, bf16[16,1024]{1,0:T(8,128)(2,1)S(1)}) custom-call(bf16[16,64,1024]{2,1,0:T(8,128)(2,1)} %refs_5_.2), custom_call_target="tpu_custom_call" | custom-call | tf_op jit(solution)/shard_map/edges/pallas_call | solution.py:285
  1.5 1.9 %collective-permute-start = (bf16[64,1024]{1,0:T(8,128)(2,1)S(1)}, bf16[64,1024]{1,0:T(8,128)(2,1)S(1)}, u32[]{:S(2)}, u32[]{:S(2)}) collective-permute-start(bf16[64,1024]{1,0:T(8,128)(2,1)S(1)} %get-tuple-element.18), channel_id=1, source_target_pairs={{0,8},{8,0},{16,24},{24,16},{32,40},{40,32},{48,56},{56,48},{64,72... | collective-permute-start | bytes 393224 | tf_op jit(solution)/shard_map/ppermute | solution.py:304
  3.4 2.0 %collective-permute-start.1 = (bf16[64,1024]{1,0:T(8,128)(2,1)S(1)}, bf16[64,1024]{1,0:T(8,128)(2,1)S(1)}, u32[]{:S(2)}, u32[]{:S(2)}) collective-permute-start(bf16[64,1024]{1,0:T(8,128)(2,1)S(1)} %get-tuple-element.19), channel_id=1, source_target_pairs={{0,248},{8,16},{16,8},{24,32},{32,24},{40,48},{48,40},{56,64},{64,... | collective-permute-start | bytes 393224 | tf_op jit(solution)/shard_map/ppermute | solution.py:304
  5.4 0.0 collective-permute-start.2
  5.4 2.9 %collective-permute-start.3 = (bf16[16,1024]{1,0:T(8,128)(2,1)S(1)}, bf16[16,1024]{1,0:T(8,128)(2,1)S(1)}, u32[]{:S(2)}, u32[]{:S(2)}) collective-permute-start(bf16[16,1024]{1,0:T(8,128)(2,1)S(1)} %get-tuple-element.21), channel_id=1, source_target_pairs={{0,7},{1,2},{2,1},{3,4},{4,3},{5,6},{6,5},{7,0},{8,15},{9,10},{10,... | collective-permute-start | bytes 98312 | tf_op jit(solution)/shard_map/ppermute | solution.py:304
  8.3 0.0 copy-done
  8.3 0.0 copy-done.5
  8.3 0.0 copy-done.1
  8.3 0.0 copy-done.4
  8.3 0.0 copy-done.3
  8.3 0.0 copy-done.2
  8.3 7.9 %interior.1.refs_10_ = f32[8,4,48,128]{3,2,1,0:T(8,128)S(1)} custom-call(f32[4]{0:T(128)S(1)} %copy-done.2, f32[4]{0:T(128)S(1)} %copy-done.3, f32[4]{0:T(128)S(1)} %copy-done.4, f32[3,4]{1,0:T(4,128)S(1)} %copy-done.1, f32[3]{0:T(128)S(1)} %copy-done.5, bf16[16,64,1024]{2,1,0:T(8,128)(2,1)S(1)} %copy-done), custom_call_target="tpu_custom_call" | custom-call | flops 60000000 | bytes 3000000 | tf_op jit(solution)/shard_map/interior/pallas_call | solution.py:312
  16.2 0.0 collective-permute-done.2.refs_8_
  16.2 0.0 collective-permute-done.3.refs_9_
  16.3 0.0 collective-permute-done.refs_6_
  16.3 0.0 collective-permute-done.1.refs_7_
  16.3 5.0 %border.1 = bf16[32,64,128]{2,1,0:T(8,128)(2,1)S(1)} custom-call(f32[4]{0:T(128)S(1)} %copy-done.2, f32[4]{0:T(128)S(1)} %copy-done.3, f32[4]{0:T(128)S(1)} %copy-done.4, f32[3,4]{1,0:T(4,128)S(1)} %copy-done.1, f32[3]{0:T(128)S(1)} %copy-done.5, bf16[16,64,1024]{2,1,0:T(8,128)(2,1)S(1)} %copy-done, bf16[64,1024]{1,0:T(8,128)(2,1)S(1)} %collective-permute-done.refs_6_, ...), custom_call_target="tpu_custom_call" | custom-call | tf_op jit(solution)/shard_map/border/pallas_call | solution.py:322
  21.3 25.4 %all_to_all.5.bricks = bf16[32,64,128]{2,1,0:T(8,128)(2,1)S(1)} all-to-all(bf16[32,64,128]{2,1,0:T(8,128)(2,1)S(1)} %border.1), channel_id=1, replica_groups=mesh['depth'=32,'rows'=8] {'depth'}, dimensions={0} | all-to-all | bytes 1048576 | tf_op jit(solution)/shard_map/all_to_all | solution.py:331
  46.7 1.2 %compose.1 = f32[4,32,64]{2,1,0:T(8,128)} custom-call(bf16[32,64,128]{2,1,0:T(8,128)(2,1)S(1)} %all_to_all.5.bricks), custom_call_target="tpu_custom_call" | custom-call | tf_op jit(solution)/shard_map/compose/pallas_call | solution.py:332
Async XLA Ops:
  0.0 8.3 %copy-start = (bf16[16,64,1024]{2,1,0:T(8,128)(2,1)S(1)}, bf16[16,64,1024]{2,1,0:T(8,128)(2,1)}, u32[]{:S(2)}) copy-start(bf16[16,64,1024]{2,1,0:T(8,128)(2,1)} %refs_5_.2) | copy-start | bytes 6291460
  0.0 8.3 %copy-start.5 = (f32[3]{0:T(128)S(1)}, f32[3]{0:T(128)}, u32[]{:S(2)}) copy-start(f32[3]{0:T(128)} %refs_4_.3) | copy-start | bytes 40
  0.0 8.3 %copy-start.1 = (f32[3,4]{1,0:T(4,128)S(1)}, f32[3,4]{1,0:T(4,128)}, u32[]{:S(2)}) copy-start(f32[3,4]{1,0:T(4,128)} %refs_3_.3) | copy-start | bytes 148
  0.0 8.3 %copy-start.4 = (f32[4]{0:T(128)S(1)}, f32[4]{0:T(128)}, u32[]{:S(2)}) copy-start(f32[4]{0:T(128)} %refs_2_.3) | copy-start | bytes 52
  0.0 8.3 %copy-start.3 = (f32[4]{0:T(128)S(1)}, f32[4]{0:T(128)}, u32[]{:S(2)}) copy-start(f32[4]{0:T(128)} %refs_1_.3) | copy-start | bytes 52
  0.0 8.3 %copy-start.2 = (f32[4]{0:T(128)S(1)}, f32[4]{0:T(128)}, u32[]{:S(2)}) copy-start(f32[4]{0:T(128)} %refs_0_.3) | copy-start | bytes 52
  1.5 14.8 %collective-permute-start = (bf16[64,1024]{1,0:T(8,128)(2,1)S(1)}, bf16[64,1024]{1,0:T(8,128)(2,1)S(1)}, u32[]{:S(2)}, u32[]{:S(2)}) collective-permute-start(bf16[64,1024]{1,0:T(8,128)(2,1)S(1)} %get-tuple-element.18), channel_id=1, source_target_pairs={{0,8},{8,0},{16,24},{24,16},{32,40},{40,32},{48,56},{56,48},{64,72... | collective-permute-start | bytes 393224 | tf_op jit(solution)/shard_map/ppermute | solution.py:304
  3.4 12.9 %collective-permute-start.1 = (bf16[64,1024]{1,0:T(8,128)(2,1)S(1)}, bf16[64,1024]{1,0:T(8,128)(2,1)S(1)}, u32[]{:S(2)}, u32[]{:S(2)}) collective-permute-start(bf16[64,1024]{1,0:T(8,128)(2,1)S(1)} %get-tuple-element.19), channel_id=1, source_target_pairs={{0,248},{8,16},{16,8},{24,32},{32,24},{40,48},{48,40},{56,64},{64,... | collective-permute-start | bytes 393224 | tf_op jit(solution)/shard_map/ppermute | solution.py:304
  5.4 10.8 %collective-permute-start.2 = (bf16[16,1024]{1,0:T(8,128)(2,1)S(1)}, bf16[16,1024]{1,0:T(8,128)(2,1)S(1)}, u32[]{:S(2)}, u32[]{:S(2)}) collective-permute-start(bf16[16,1024]{1,0:T(8,128)(2,1)S(1)} %get-tuple-element.20), channel_id=1, source_target_pairs={{0,1},{1,0},{2,3},{3,2},{4,5},{5,4},{6,7},{7,6},{8,9},{9,8},{10,11... | collective-permute-start | bytes 98312 | tf_op jit(solution)/shard_map/ppermute | solution.py:304
  5.4 10.8 %collective-permute-start.3 = (bf16[16,1024]{1,0:T(8,128)(2,1)S(1)}, bf16[16,1024]{1,0:T(8,128)(2,1)S(1)}, u32[]{:S(2)}, u32[]{:S(2)}) collective-permute-start(bf16[16,1024]{1,0:T(8,128)(2,1)S(1)} %get-tuple-element.21), channel_id=1, source_target_pairs={{0,7},{1,2},{2,1},{3,4},{4,3},{5,6},{6,5},{7,0},{8,15},{9,10},{10,... | collective-permute-start | bytes 98312 | tf_op jit(solution)/shard_map/ppermute | solution.py:304

commit v5 on v4

v5 whole, which is shorter than its diff:
```python
import math

import jax
import jax.numpy as jnp
from jax import lax
from jax.experimental import pallas as pl
from jax.experimental.pallas import tpu as pltpu
from jax.sharding import PartitionSpec as P

LOG2E = math.log2(math.e)
TILE = 16
LANES = 128
BAND = 32
MB = 1024 * 1024


def dither(brick, shape):
    lane = lax.broadcasted_iota(jnp.int32, shape, 1)
    row = lax.broadcasted_iota(jnp.int32, shape, 0)
    phase = (lane * 29 + row * 13 + brick * 37) & 63
    return phase.astype(jnp.float32) * (1.0 / 64.0) + 1.0


def edges_kernel(field, plane_one, plane_two, row_one, row_two, tiles, gathered, sems):
    depth, rows, _ = field.shape
    chosen = jnp.where((lax.axis_index("depth") & 1) == 0, depth - 1, 0)
    copies = [
        pltpu.make_async_copy(field.at[:, 0:TILE], tiles.at[0], sems.at[0]),
        pltpu.make_async_copy(field.at[:, rows - TILE : rows], tiles.at[1], sems.at[1]),
        pltpu.make_async_copy(field.at[chosen], plane_one, sems.at[2]),
        pltpu.make_async_copy(field.at[depth - 1 - chosen], plane_two, sems.at[3]),
    ]
    for copy in copies:
        copy.start()
    for side, row in ((0, 0), (1, TILE - 1)):
        copies[side].wait()
        for plane in range(depth):
            tile = tiles[side, plane].astype(jnp.float32)
            gathered[side, plane : plane + 1, :] = tile[row : row + 1, :]
    even = (lax.axis_index("rows") & 1) == 0
    row_one[...] = jnp.where(even, gathered[1], gathered[0]).astype(jnp.bfloat16)
    row_two[...] = jnp.where(even, gathered[0], gathered[1]).astype(jnp.bfloat16)
    copies[2].wait()
    copies[3].wait()


def start_params(sources, targets, sems):
    copies = [
        pltpu.make_async_copy(source, target, sems.at[i]) for i, (source, target) in enumerate(zip(sources, targets))
    ]
    for copy in copies:
        copy.start()
    return copies


def shader(step_size, cells, centers, widths, density, colors, light):
    def full(scalar):
        return jnp.full((8, LANES), scalar, jnp.float32)

    count = centers.shape[0]
    center = [full(centers[k]) for k in range(count)]
    sharp = [-LOG2E / (full(widths[k]) * full(widths[k])) for k in range(count)]
    dense = [full(density[k]) * (-4.0 * LOG2E * step_size) for k in range(count)]
    lights = [full(light[k]) for k in range(3)]
    length = lax.rsqrt(lights[0] * lights[0] + lights[1] * lights[1] + lights[2] * lights[2])
    lights = [component * length * 0.7 for component in lights]
    lane = lax.broadcasted_iota(jnp.int32, (8, LANES), 1)
    at_first, at_last = lane == 0, lane == LANES - 1

    def rows_at(start):
        return pl.ds(pl.multiple_of(start + 8, 8), 8)

    def enter(j, start, plane, total=None, sums=None):
        zero = jnp.zeros((8, LANES), jnp.float32)
        before, at = cells[j + 1, plane, rows_at(start), :], cells[j + 1, plane + 1, rows_at(start), :]
        if total is None:
            return [before, at, zero, jnp.ones((8, LANES), jnp.float32)] + [zero] * count
        return [before, at, total, jnp.exp2(total)] + sums

    def step(j, start, plane, state):
        previous, current, total, clear, *sums = state
        here = rows_at(start)
        following = cells[j + 1, plane + 2, here, :]
        dz = following - previous
        dy = cells[j + 1, plane + 1, pl.ds(start + 9, 8), :] - cells[j + 1, plane + 1, pl.ds(start + 7, 8), :]
        dx = pltpu.roll(
            jnp.where(at_first, cells[j + 2, plane + 1, here, :], current), LANES - 1, 1
        ) - pltpu.roll(jnp.where(at_last, cells[j, plane + 1, here, :], current), 1, 1)
        root = lax.rsqrt(dz * dz + dy * dy + dx * dx + 4.0)
        lighting = 0.3 + jnp.abs(dz * lights[0] + dy * lights[1] + dx * lights[2]) * root
        bumps = []
        for k in range(count):
            offset = current - center[k]
            bumps.append(jnp.exp2(offset * offset * sharp[k]))
        sigma = dense[0] * bumps[0]
        weight = bumps[0] + 0.1
        for k in range(1, count):
            sigma = sigma + dense[k] * bumps[k]
            weight = weight + bumps[k]
        total = total + sigma * (0.3125 - root * root)
        remaining = jnp.exp2(total)
        factor = (clear - remaining) * lighting * pl.reciprocal(weight)
        sums = [s + factor * b for s, b in zip(sums, bumps)]
        return [current, following, total, remaining] + sums

    def mix(sums):
        mixed = []
        for c in range(3):
            colour = colors[c, 0] * sums[0]
            for k in range(1, count):
                colour = colour + colors[c, k] * sums[k]
            mixed.append(colour)
        return mixed

    return enter, step, mix


def spread(cells, plane, first, tile):
    for j in range(tile.shape[1] // LANES):
        cells[j + 1, plane, pl.ds(pl.multiple_of(8 + first, 8), TILE), :] = tile[:, LANES * j : LANES * (j + 1)]


def is_even(axis):
    return (lax.axis_index(axis) & 1) == 0


def strips_of(upper_half, rows):
    outer = jnp.where(upper_half, 0, rows - 8)
    inner = jnp.where(upper_half, 8, rows // 2)
    return [outer] + [inner + 8 * i for i in range(rows // 16 - 1)]


def tiles_of(upper_half, rows):
    base = jnp.where(upper_half, 0, rows // 2 - TILE)
    return [base + TILE * i for i in range(rows // 2 // TILE + 1)]


def zero_sides(cells, upper_half, depth, rows, lanes):
    half = pl.ds(pl.multiple_of(8 + jnp.where(upper_half, 0, rows // 2), 8), rows // 2)
    for side in (0, lanes + 1):
        for plane in range(depth):
            cells[side, plane + 1, half, :] = jnp.zeros((rows // 2, LANES), jnp.float32)


def load_tile(field, cells, plane, first):
    part = field[plane, pl.ds(pl.multiple_of(first, TILE), TILE), :]
    spread(cells, plane + 1, first, part.astype(jnp.float32))


def load_halos(
    cells, plane_one, plane_two, row_one, row_two, upper_half, depth_count, row_count, depth, rows, lanes
):
    def sided(axis, count):
        index = lax.axis_index(axis)
        return is_even(axis), (index > 0).astype(jnp.float32), (index < count - 1).astype(jnp.float32)

    def around(one, two, even, keep_lo, keep_hi):
        one, two = one.astype(jnp.float32), two.astype(jnp.float32)
        return jnp.where(even, two, one) * keep_lo, jnp.where(even, one, two) * keep_hi

    plane_sides, row_sides = sided("depth", depth_count), sided("rows", row_count)
    for first in tiles_of(upper_half, rows):
        part = pl.ds(pl.multiple_of(first, TILE), TILE)
        low, high = around(plane_one[part, :], plane_two[part, :], *plane_sides)
        spread(cells, 0, first, low)
        spread(cells, depth + 1, first, high)
    low, high = around(row_one[...], row_two[...], *row_sides)
    beside, line = jnp.where(upper_half, low, high), pl.ds(jnp.where(upper_half, 7, 8 + rows), 1)
    for j in range(lanes):
        for plane in range(depth):
            cells[j + 1, plane + 1, line, :] = beside[plane : plane + 1, LANES * j : LANES * (j + 1)]


def encode(value, scale):
    value = value * scale
    value = value * value
    value = value * value
    return (value * value).astype(jnp.bfloat16)


def decode(coded, unscale):
    return jnp.exp(jnp.log(coded.astype(jnp.float32)) * 0.125) * unscale


def early_kernel(step_size, *refs):
    param_sources, field, out, cells, params, sems = refs[:5], refs[5], refs[6], refs[7], refs[8:13], refs[13]
    depth, rows, width = field.shape
    lanes = width // LANES
    smalls = start_params(param_sources, params, sems)
    send_upper = jnp.logical_not(is_even("depth"))
    zero_sides(cells, send_upper, depth, rows, lanes)
    firsts = tiles_of(send_upper, rows)

    def prepare(plane, carry):
        for first in firsts:
            load_tile(field, cells, plane, first)
        return carry

    lax.fori_loop(0, depth, prepare, 0)
    for copy in smalls:
        copy.wait()
    enter, step, mix = shader(step_size, cells, *params)
    starts = strips_of(send_upper, rows)[1:]

    def march(j, carry):
        states = [enter(j, start, 1) for start in starts]
        for plane in range(1, depth - 1):
            states = [step(j, start, plane, state) for start, state in zip(starts, states)]
        for i, state in enumerate(states):
            for c, value in enumerate(mix(state[4:]) + [state[2]]):
                out[j, c, 8 * i : 8 * i + 8, :] = value
        return carry

    lax.fori_loop(0, lanes, march, 0)


def send_kernel(step_size, depth_count, row_count, *refs):
    param_sources, field, plane_one, plane_two, row_one, row_two, early, out = refs[:5], *refs[5:12]
    cells, params, sems = refs[12], refs[13:18], refs[18]
    depth, rows, width = field.shape
    lanes = width // LANES
    smalls = start_params(param_sources, params, sems)
    send_upper = jnp.logical_not(is_even("depth"))
    zero_sides(cells, send_upper, depth, rows, lanes)
    firsts = tiles_of(send_upper, rows)
    load_halos(cells, plane_one, plane_two, row_one, row_two, send_upper, depth_count, row_count, depth, rows, lanes)
    outer = jnp.where(send_upper, 0, rows - TILE)

    def prepare(plane, carry):
        load_tile(field, cells, plane, outer)
        return carry

    lax.fori_loop(0, depth, prepare, 0)
    for plane in (0, 1, depth - 2, depth - 1):
        for first in firsts:
            load_tile(field, cells, plane, first)
    for copy in smalls:
        copy.wait()
    enter, step, mix = shader(step_size, cells, *params)
    starts = strips_of(send_upper, rows)
    scale = dither(lax.axis_index("depth"), (TILE, LANES)) * 65536.0

    def march(j, carry):
        state = enter(j, starts[0], 0)
        for plane in range(depth):
            state = step(j, starts[0], plane, state)
        strips = [mix(state[4:]) + [-state[2]]]
        for i, start in enumerate(starts[1:]):
            state = step(j, start, 0, enter(j, start, 0))
            front, total = state[3], state[2] + early[j, 3, 8 * i : 8 * i + 8, :]
            state = step(j, start, depth - 1, enter(j, start, depth - 1, total, state[4:]))
            values = [v + front * early[j, c, 8 * i : 8 * i + 8, :] for c, v in enumerate(mix(state[4:]))]
            strips.append(values + [-state[2]])
        for c in range(4):
            for i in range(0, len(strips), 2):
                both = jnp.concatenate([strips[i][c], strips[i + 1][c]], axis=0)
                out[j, c, 8 * i : 8 * i + 16, :] = encode(both, scale)
        return carry

    lax.fori_loop(0, lanes, march, 0)


def keep_kernel(step_size, depth_count, row_count, *refs):
    param_sources, field, plane_one, plane_two, row_one, row_two, out = refs[:5], *refs[5:11]
    cells, params, sems = refs[11], refs[12:17], refs[17]
    depth, rows, width = field.shape
    lanes = width // LANES
    smalls = start_params(param_sources, params, sems)
    keep_upper = is_even("depth")
    zero_sides(cells, keep_upper, depth, rows, lanes)
    firsts = tiles_of(keep_upper, rows)
    load_halos(cells, plane_one, plane_two, row_one, row_two, keep_upper, depth_count, row_count, depth, rows, lanes)

    def prepare(plane, carry):
        for first in firsts:
            load_tile(field, cells, plane, first)
        return carry

    lax.fori_loop(0, depth, prepare, 0)
    for copy in smalls:
        copy.wait()
    enter, step, mix = shader(step_size, cells, *params)
    starts = strips_of(keep_upper, rows)

    def march(j, carry):
        done = []
        for i in range(0, len(starts), 2):
            pair = starts[i : i + 2]
            states = [enter(j, start, 0) for start in pair]
            for plane in range(depth):
                states = [step(j, start, plane, state) for start, state in zip(pair, states)]
            done += [mix(state[4:]) + [-state[2]] for state in states]
        for i, values in enumerate(done):
            for c in range(4):
                out[j, c, 8 * i : 8 * i + 8, :] = values[c]
        return carry

    lax.fori_loop(0, lanes, march, 0)


def join_kernel(own, other, out):
    lanes = own.shape[0]
    me, even = lax.axis_index("depth"), is_even("depth")
    unscale = 1.0 / (dither(me + 1 - 2 * (me & 1), (TILE, LANES)) * 65536.0)
    scale = dither(me, (TILE, LANES)) * 32768.0
    lane = lax.broadcasted_iota(jnp.int32, (8, LANES), 1)
    upper, odd = lane >= 64, (lane & BAND) > 0

    def exchange(a, b, mask, shift):
        moved = pltpu.roll(jnp.where(mask, a, b), shift, 1)
        return jnp.where(mask, moved, a), jnp.where(mask, b, moved)

    def one(j):
        bands = [[], [], [], []]
        joined = [[] for _ in range(4)]
        for half in range(2):
            part = slice(TILE * half, TILE * (half + 1))
            mine = [own[j, c, part, :] for c in range(4)]
            theirs = [decode(other[j, c, part, :], unscale) for c in range(4)]
            front = jnp.exp2(-jnp.where(even, mine[3], theirs[3]))
            for c in range(3):
                first, second = jnp.where(even, mine[c], theirs[c]), jnp.where(even, theirs[c], mine[c])
                joined[c].append(first + front * second)
            joined[3].append(mine[3] + theirs[3])
        for c in range(4):
            strip = [joined[c][i // 2][8 * (i % 2) : 8 * (i % 2) + 8, :] for i in range(4)]
            strip[0], strip[2] = exchange(strip[0], strip[2], upper, 64)
            strip[1], strip[3] = exchange(strip[1], strip[3], upper, 64)
            strip[0], strip[1] = exchange(strip[0], strip[1], odd, BAND)
            strip[2], strip[3] = exchange(strip[2], strip[3], odd, BAND)
            for band in range(4):
                bands[band].append(strip[band])
        for band in range(4):
            for c in (0, 2):
                both = jnp.concatenate([bands[band][c], bands[band][c + 1]], axis=0)
                out[4 * j + band, 8 * c : 8 * c + 16, :] = encode(both, scale)

    for j in range(lanes):
        one(j)


def compose_kernel(bricks, out):
    count = bricks.shape[0]
    halves = []
    for half in range(2):
        total = jnp.zeros((8, LANES), jnp.float32)
        image = [jnp.zeros((8, LANES), jnp.float32) for _ in range(3)]
        for brick in range(half, count, 2):
            unscale = 1.0 / (dither(brick, (TILE, LANES)) * 32768.0)
            values = []
            for c in (0, 2):
                both = decode(bricks[brick, 8 * c : 8 * c + 16, :], unscale)
                values += [both[:8], both[8:]]
            front = jnp.exp2(-total)
            image = [sofar + front * value for sofar, value in zip(image, values)]
            total = total + values[3]
        halves.append(image + [1.0 - jnp.exp2(-total)])
    odd = jnp.logical_not(is_even("depth"))
    for c in range(4):
        turned = jnp.concatenate([halves[0][c], halves[1][c]], axis=0).T
        block = [turned[BAND * q : BAND * (q + 1), :] for q in range(4)]
        block[0], block[2] = jnp.where(odd, block[2], block[0]), jnp.where(odd, block[0], block[2])
        out[c] = jnp.concatenate(
            [block[q][:, :8] for q in (0, 1, 2, 3)] + [block[q][:, 8:] for q in (1, 2, 3, 0)], axis=1
        )


def shards(field, tf_centers, tf_widths, tf_density, tf_colors, light):
    depth_count, row_count = lax.axis_size("depth"), lax.axis_size("rows")
    depth, rows, width = field.shape
    lanes = width // LANES
    step_size = 0.5 / (depth * depth_count)
    hbm, vmem = pl.BlockSpec(memory_space=pltpu.HBM), pl.BlockSpec(memory_space=pltpu.VMEM)

    edge = jax.ShapeDtypeStruct((rows, width), jnp.bfloat16)
    row_edge = jax.ShapeDtypeStruct((depth, width), jnp.bfloat16)
    edges = pl.pallas_call(
        edges_kernel,
        out_shape=(edge, edge, row_edge, row_edge),
        in_specs=[hbm],
        out_specs=(vmem,) * 4,
        scratch_shapes=[
            pltpu.VMEM((2, depth, TILE, width), jnp.bfloat16),
            pltpu.VMEM((2, depth, width), jnp.float32),
            pltpu.SemaphoreType.DMA((4,)),
        ],
        compiler_params=pltpu.CompilerParams(vmem_limit_bytes=52 * MB),
        name="edges",
    )(field)

    inner_field, *edges = lax.optimization_barrier((field, *edges))

    def exchange(one, two, axis, count):
        near = [(k, k ^ 1) for k in range(count)]
        far = [(k, (k - 1 + 2 * (k & 1)) % count) for k in range(count)]
        return lax.ppermute(one, axis, near), lax.ppermute(two, axis, far)

    plane_one, plane_two = exchange(edges[0], edges[1], "depth", depth_count)
    row_one, row_two = exchange(edges[2], edges[3], "rows", row_count)

    params = (tf_centers, tf_widths, tf_density, tf_colors, light)
    cells = pltpu.VMEM((lanes + 2, depth + 2, rows + 16, LANES), jnp.float32)
    param_scratch = [pltpu.SMEM(param.shape, jnp.float32) for param in params] + [pltpu.SemaphoreType.DMA((5,))]
    scratch = [cells] + param_scratch
    compiler_params = pltpu.CompilerParams(vmem_limit_bytes=32 * MB)
    early = pl.pallas_call(
        lambda *refs: early_kernel(step_size, *refs),
        out_shape=jax.ShapeDtypeStruct((lanes, 4, rows // 2 - 8, LANES), jnp.float32),
        in_specs=[hbm] * 5 + [vmem],
        out_specs=vmem,
        scratch_shapes=scratch,
        compiler_params=compiler_params,
        cost_estimate=pl.CostEstimate(flops=30_000_000, bytes_accessed=3_000_000, transcendentals=3_000_000),
        name="early",
    )(*params, inner_field)
    halos = (plane_one, plane_two, row_one, row_two)
    half = (lanes, 4, rows // 2, LANES)
    sent = pl.pallas_call(
        lambda *refs: send_kernel(step_size, depth_count, row_count, *refs),
        out_shape=jax.ShapeDtypeStruct(half, jnp.bfloat16),
        in_specs=[hbm] * 5 + [vmem] * 6,
        out_specs=vmem,
        scratch_shapes=scratch,
        compiler_params=compiler_params,
        name="send",
    )(*params, field, *halos, early)
    keep_field, sent = lax.optimization_barrier((field, sent))
    other = lax.ppermute(sent, "depth", [(k, k ^ 1) for k in range(depth_count)])
    own = pl.pallas_call(
        lambda *refs: keep_kernel(step_size, depth_count, row_count, *refs),
        out_shape=jax.ShapeDtypeStruct(half, jnp.float32),
        in_specs=[hbm] * 5 + [vmem] * 5,
        out_specs=vmem,
        scratch_shapes=scratch,
        compiler_params=compiler_params,
        cost_estimate=pl.CostEstimate(flops=50_000_000, bytes_accessed=3_000_000, transcendentals=4_000_000),
        name="keep",
    )(*params, keep_field, *halos)
    bricks = pl.pallas_call(
        join_kernel,
        out_shape=jax.ShapeDtypeStruct((width // BAND, rows // 2, LANES), jnp.bfloat16),
        in_specs=[vmem, vmem],
        out_specs=vmem,
        compiler_params=compiler_params,
        name="join",
    )(own, other)
    bricks = lax.all_to_all(bricks, "depth", 0, 0, tiled=True)
    image = pl.pallas_call(
        compose_kernel,
        out_shape=jax.ShapeDtypeStruct((4, width // depth_count, rows), jnp.float32),
        in_specs=[vmem],
        out_specs=vmem,
        compiler_params=pltpu.CompilerParams(vmem_limit_bytes=16 * MB),
        name="compose",
    )(bricks)
    return jnp.transpose(image, (0, 2, 1))


def solution(mesh):
    placed = (P("depth", "rows", None), P(), P(), P(), P(), P())
    return jax.shard_map(
        shards, mesh=mesh, in_specs=placed, out_specs=P(None, "rows", "depth"), check_vma=False
    )
```

time: 48 us -> 45.8 us (0.954)
  the two profiles are of different devices: /device:TPU:32 before, /device:TPU:2 now
where the time goes in v5:
time: 45.8 us; the launch traced here: 45.7 us
  blocking collectives  16.3 us (36%)
  Pallas kernels  15.9 us (35%)
  starting transfers between devices  10.1 us (22%)
  waiting for transfers between devices  3.13 us (7%)
    all_to_all x1, blocking collectives, shards(): bricks = lax.all_to_all(bricks, 'depth', 0, 0, tiled=True)  16.3 us
    ppermute x4, starting transfers between devices, exchange(): return (lax.ppermute(one, axis, near), lax.ppermute(two, axis, far))  10.1 us
    pallas_call x1, Pallas kernels, shards(): pl.pallas_call(lambda *refs: keep_kernel(step_size, depth_count, row_coun...  6.03 us
    pallas_call x1, Pallas kernels, shards(): pl.pallas_call(lambda *refs: early_kernel(step_size, *refs), out_shape=ja...  4.13 us
    ppermute x1, waiting for transfers between devices, shards(): lax.ppermute(sent, 'depth', [(k, k ^ 1) for k in range(depth_count)])  3.12 us
    pallas_call x1, Pallas kernels, shards(): pl.pallas_call(lambda *refs: send_kernel(step_size, depth_count, row_coun...  2.72 us
    pallas_call x1, Pallas kernels, shards(): pl.pallas_call(edges_kernel, out_shape=(edge, edge, row_edge, row_edge),...  1.44 us
    pallas_call x1, Pallas kernels, shards(): pl.pallas_call(compose_kernel, out_shape=jax.ShapeDtypeStruct((4, width /...  1.17 us
  transfers between devices with their start and end apart: 5, of which 1 were waited for; matrix products, arithmetic and copies ran while one was open for 0% of the time, Pallas kernels for 22%

profile of v5, /device:TPU:2, one launch (start us, length us, event | category | flops | bytes accessed | tf_op | source)
XLA Modules:
  0.0 45.7 jit_solution(16534446115679038347)
XLA Ops:
  0.0 0.0 copy-start
  0.0 0.0 copy-start.5
  0.0 0.0 copy-start.1
  0.0 0.0 copy-start.4
  0.0 0.0 copy-start.3
  0.0 0.0 copy-start.2
  0.0 1.4 %edges.1 = (bf16[64,1024]{1,0:T(8,128)(2,1)S(1)}, bf16[64,1024]{1,0:T(8,128)(2,1)S(1)}, bf16[16,1024]{1,0:T(8,128)(2,1)S(1)}, bf16[16,1024]{1,0:T(8,128)(2,1)S(1)}) custom-call(bf16[16,64,1024]{2,1,0:T(8,128)(2,1)} %refs_5_.3), custom_call_target="tpu_custom_call" | custom-call | tf_op jit(solution)/shard_map/edges/pallas_call | solution.py:377
  1.5 2.0 %collective-permute-start = (bf16[64,1024]{1,0:T(8,128)(2,1)S(1)}, bf16[64,1024]{1,0:T(8,128)(2,1)S(1)}, u32[]{:S(2)}, u32[]{:S(2)}) collective-permute-start(bf16[64,1024]{1,0:T(8,128)(2,1)S(1)} %get-tuple-element.20), channel_id=1, source_target_pairs={{0,8},{8,0},{16,24},{24,16},{32,40},{40,32},{48,56},{56,48},{64,72... | collective-permute-start | bytes 393224 | tf_op jit(solution)/shard_map/ppermute | solution.py:396
  3.5 7.4 %collective-permute-start.1 = (bf16[64,1024]{1,0:T(8,128)(2,1)S(1)}, bf16[64,1024]{1,0:T(8,128)(2,1)S(1)}, u32[]{:S(2)}, u32[]{:S(2)}) collective-permute-start(bf16[64,1024]{1,0:T(8,128)(2,1)S(1)} %get-tuple-element.21), channel_id=1, source_target_pairs={{0,248},{8,16},{16,8},{24,32},{32,24},{40,48},{48,40},{56,64},{64,... | collective-permute-start | bytes 393224 | tf_op jit(solution)/shard_map/ppermute | solution.py:396
  10.9 0.0 collective-permute-start.2
  10.9 0.6 %collective-permute-start.3 = (bf16[16,1024]{1,0:T(8,128)(2,1)S(1)}, bf16[16,1024]{1,0:T(8,128)(2,1)S(1)}, u32[]{:S(2)}, u32[]{:S(2)}) collective-permute-start(bf16[16,1024]{1,0:T(8,128)(2,1)S(1)} %get-tuple-element.23), channel_id=1, source_target_pairs={{0,7},{1,2},{2,1},{3,4},{4,3},{5,6},{6,5},{7,0},{8,15},{9,10},{10,... | collective-permute-start | bytes 98312 | tf_op jit(solution)/shard_map/ppermute | solution.py:396
  11.5 0.0 copy-done
  11.5 0.0 copy-done.5
  11.5 0.0 copy-done.1
  11.5 0.0 copy-done.4
  11.6 0.0 copy-done.3
  11.6 0.0 copy-done.2
  11.6 4.1 %early.1.refs_10_ = f32[8,4,24,128]{3,2,1,0:T(8,128)S(1)} custom-call(f32[4]{0:T(128)S(1)} %copy-done.2, f32[4]{0:T(128)S(1)} %copy-done.3, f32[4]{0:T(128)S(1)} %copy-done.4, f32[3,4]{1,0:T(4,128)S(1)} %copy-done.1, f32[3]{0:T(128)S(1)} %copy-done.5, bf16[16,64,1024]{2,1,0:T(8,128)(2,1)S(1)} %copy-done), custom_call_target="tpu_custom_call" | custom-call | flops 30000000 | bytes 3000000 | tf_op jit(solution)/shard_map/early/pallas_call | solution.py:406
  15.7 0.0 collective-permute-done.2.refs_8_
  15.7 0.0 collective-permute-done.3.refs_9_
  15.7 0.0 collective-permute-done.refs_6_
  15.7 0.0 collective-permute-done.1.refs_7_
  15.8 2.7 %send.1 = bf16[8,4,32,128]{3,2,1,0:T(8,128)(2,1)S(1)} custom-call(f32[4]{0:T(128)S(1)} %copy-done.2, f32[4]{0:T(128)S(1)} %copy-done.3, f32[4]{0:T(128)S(1)} %copy-done.4, f32[3,4]{1,0:T(4,128)S(1)} %copy-done.1, f32[3]{0:T(128)S(1)} %copy-done.5, bf16[16,64,1024]{2,1,0:T(8,128)(2,1)S(1)} %copy-done, bf16[64,1024]{1,0:T(8,128)(2,1)S(1)} %collective-permute-done.refs_6_, ...), custom_call_target="tpu_custom_call" | custom-call | tf_op jit(solution)/shard_map/send/pallas_call | solution.py:418
  18.5 0.1 collective-permute-start.4
  18.6 6.0 %keep.1.own = f32[8,4,32,128]{3,2,1,0:T(8,128)S(1)} custom-call(f32[4]{0:T(128)S(1)} %copy-done.2, f32[4]{0:T(128)S(1)} %copy-done.3, f32[4]{0:T(128)S(1)} %copy-done.4, f32[3,4]{1,0:T(4,128)S(1)} %copy-done.1, f32[3]{0:T(128)S(1)} %copy-done.5, bf16[16,64,1024]{2,1,0:T(8,128)(2,1)S(1)} %copy-done, bf16[64,1024]{1,0:T(8,128)(2,1)S(1)} %collective-permute-done.refs_6_, ...), custom_call_target="tpu_custom_call" | custom-call | flops 50000000 | bytes 3000000 | tf_op jit(solution)/shard_map/keep/pallas_call | solution.py:429
  24.6 3.1 %collective-permute-done.4.other = bf16[8,4,32,128]{3,2,1,0:T(8,128)(2,1)S(1)} collective-permute-done((bf16[8,4,32,128]{3,2,1,0:T(8,128)(2,1)S(1)}, bf16[8,4,32,128]{3,2,1,0:T(8,128)(2,1)S(1)}, u32[]{:S(2)}, u32[]{:S(2)}) %collective-permute-start.4) | collective-permute-done | bytes 262176 | tf_op jit(solution)/shard_map/ppermute | solution.py:428
  27.7 0.4 join.1
  28.2 16.3 %all_to_all.5.bricks = bf16[32,32,128]{2,1,0:T(8,128)(2,1)S(1)} all-to-all(bf16[32,32,128]{2,1,0:T(8,128)(2,1)S(1)} %join.1), channel_id=1, replica_groups=mesh['depth'=32,'rows'=8] {'depth'}, dimensions={0} | all-to-all | bytes 524288 | tf_op jit(solution)/shard_map/all_to_all | solution.py:447
  44.5 1.2 %compose.1 = f32[4,32,64]{2,1,0:T(8,128)} custom-call(bf16[32,32,128]{2,1,0:T(8,128)(2,1)S(1)} %all_to_all.5.bricks), custom_call_target="tpu_custom_call" | custom-call | tf_op jit(solution)/shard_map/compose/pallas_call | solution.py:448
Async XLA Ops:
  0.0 11.5 %copy-start = (bf16[16,64,1024]{2,1,0:T(8,128)(2,1)S(1)}, bf16[16,64,1024]{2,1,0:T(8,128)(2,1)}, u32[]{:S(2)}) copy-start(bf16[16,64,1024]{2,1,0:T(8,128)(2,1)} %refs_5_.3) | copy-start | bytes 6291460
  0.0 11.5 %copy-start.5 = (f32[3]{0:T(128)S(1)}, f32[3]{0:T(128)}, u32[]{:S(2)}) copy-start(f32[3]{0:T(128)} %refs_4_.5) | copy-start | bytes 40
  0.0 11.5 %copy-start.1 = (f32[3,4]{1,0:T(4,128)S(1)}, f32[3,4]{1,0:T(4,128)}, u32[]{:S(2)}) copy-start(f32[3,4]{1,0:T(4,128)} %refs_3_.5) | copy-start | bytes 148
  0.0 11.5 %copy-start.4 = (f32[4]{0:T(128)S(1)}, f32[4]{0:T(128)}, u32[]{:S(2)}) copy-start(f32[4]{0:T(128)} %refs_2_.5) | copy-start | bytes 52
  0.0 11.5 %copy-start.3 = (f32[4]{0:T(128)S(1)}, f32[4]{0:T(128)}, u32[]{:S(2)}) copy-start(f32[4]{0:T(128)} %refs_1_.5) | copy-start | bytes 52
  0.0 11.5 %copy-start.2 = (f32[4]{0:T(128)S(1)}, f32[4]{0:T(128)}, u32[]{:S(2)}) copy-start(f32[4]{0:T(128)} %refs_0_.5) | copy-start | bytes 52
  1.5 14.2 %collective-permute-start = (bf16[64,1024]{1,0:T(8,128)(2,1)S(1)}, bf16[64,1024]{1,0:T(8,128)(2,1)S(1)}, u32[]{:S(2)}, u32[]{:S(2)}) collective-permute-start(bf16[64,1024]{1,0:T(8,128)(2,1)S(1)} %get-tuple-element.20), channel_id=1, source_target_pairs={{0,8},{8,0},{16,24},{24,16},{32,40},{40,32},{48,56},{56,48},{64,72... | collective-permute-start | bytes 393224 | tf_op jit(solution)/shard_map/ppermute | solution.py:396
  3.5 12.3 %collective-permute-start.1 = (bf16[64,1024]{1,0:T(8,128)(2,1)S(1)}, bf16[64,1024]{1,0:T(8,128)(2,1)S(1)}, u32[]{:S(2)}, u32[]{:S(2)}) collective-permute-start(bf16[64,1024]{1,0:T(8,128)(2,1)S(1)} %get-tuple-element.21), channel_id=1, source_target_pairs={{0,248},{8,16},{16,8},{24,32},{32,24},{40,48},{48,40},{56,64},{64,... | collective-permute-start | bytes 393224 | tf_op jit(solution)/shard_map/ppermute | solution.py:396
  10.9 4.8 %collective-permute-start.2 = (bf16[16,1024]{1,0:T(8,128)(2,1)S(1)}, bf16[16,1024]{1,0:T(8,128)(2,1)S(1)}, u32[]{:S(2)}, u32[]{:S(2)}) collective-permute-start(bf16[16,1024]{1,0:T(8,128)(2,1)S(1)} %get-tuple-element.22), channel_id=1, source_target_pairs={{0,1},{1,0},{2,3},{3,2},{4,5},{5,4},{6,7},{7,6},{8,9},{9,8},{10,11... | collective-permute-start | bytes 98312 | tf_op jit(solution)/shard_map/ppermute | solution.py:396
  10.9 4.8 %collective-permute-start.3 = (bf16[16,1024]{1,0:T(8,128)(2,1)S(1)}, bf16[16,1024]{1,0:T(8,128)(2,1)S(1)}, u32[]{:S(2)}, u32[]{:S(2)}) collective-permute-start(bf16[16,1024]{1,0:T(8,128)(2,1)S(1)} %get-tuple-element.23), channel_id=1, source_target_pairs={{0,7},{1,2},{2,1},{3,4},{4,3},{5,6},{6,5},{7,0},{8,15},{9,10},{10,... | collective-permute-start | bytes 98312 | tf_op jit(solution)/shard_map/ppermute | solution.py:396
  18.5 9.3 %collective-permute-start.4 = (bf16[8,4,32,128]{3,2,1,0:T(8,128)(2,1)S(1)}, bf16[8,4,32,128]{3,2,1,0:T(8,128)(2,1)S(1)}, u32[]{:S(2)}, u32[]{:S(2)}) collective-permute-start(bf16[8,4,32,128]{3,2,1,0:T(8,128)(2,1)S(1)} %send.1), channel_id=1, source_target_pairs={{0,8},{8,0},{16,24},{24,16},{32,40},{40,32},{48,56},{56,48},{64,72... | collective-permute-start | bytes 786440 | tf_op jit(solution)/shard_map/ppermute | solution.py:428

commit v6 on v5

--- a/solution.py
+++ b/solution.py
@@ -179,7 +179,7 @@
 
 
 def decode(coded, unscale):
-    return jnp.exp(jnp.log(coded.astype(jnp.float32)) * 0.125) * unscale
+    return jnp.exp2(jnp.log(coded.astype(jnp.float32)) * (0.125 * LOG2E)) * unscale
 
 
 def early_kernel(step_size, *refs):
@@ -284,8 +284,8 @@
 
     def march(j, carry):
         done = []
-        for i in range(0, len(starts), 2):
-            pair = starts[i : i + 2]
+        for i in range(0, len(starts), 4):
+            pair = starts[i : i + 4]
             states = [enter(j, start, 0) for start in pair]
             for plane in range(depth):
                 states = [step(j, start, plane, state) for start, state in zip(pair, states)]

time: 45.8 us -> 45.7 us (level)
  no operation moved by 1% of the time
where the time goes in v6:
time: 45.7 us; the launch traced here: 45.6 us
  blocking collectives  16.3 us (36%)
  Pallas kernels  15.9 us (35%)
  starting transfers between devices  10.1 us (22%)
  waiting for transfers between devices  3.09 us (7%)
    all_to_all x1, blocking collectives, shards(): bricks = lax.all_to_all(bricks, 'depth', 0, 0, tiled=True)  16.3 us
    ppermute x4, starting transfers between devices, exchange(): return (lax.ppermute(one, axis, near), lax.ppermute(two, axis, far))  10.1 us
    pallas_call x1, Pallas kernels, shards(): pl.pallas_call(lambda *refs: keep_kernel(step_size, depth_count, row_coun...  6.07 us
    pallas_call x1, Pallas kernels, shards(): pl.pallas_call(lambda *refs: early_kernel(step_size, *refs), out_shape=ja...  4.13 us
    ppermute x1, waiting for transfers between devices, shards(): lax.ppermute(sent, 'depth', [(k, k ^ 1) for k in range(depth_count)])  3.08 us
    pallas_call x1, Pallas kernels, shards(): pl.pallas_call(lambda *refs: send_kernel(step_size, depth_count, row_coun...  2.72 us
    pallas_call x1, Pallas kernels, shards(): pl.pallas_call(edges_kernel, out_shape=(edge, edge, row_edge, row_edge),...  1.44 us
    pallas_call x1, Pallas kernels, shards(): pl.pallas_call(compose_kernel, out_shape=jax.ShapeDtypeStruct((4, width /...  1.16 us
  transfers between devices with their start and end apart: 5, of which 1 were waited for; matrix products, arithmetic and copies ran while one was open for 0% of the time, Pallas kernels for 22%

profile of v6, /device:TPU:2, one launch (start us, length us, event | category | flops | bytes accessed | tf_op | source)
XLA Modules:
  0.0 45.6 jit_solution(11410692366789147548)
XLA Ops:
  0.0 0.0 copy-start
  0.0 0.0 copy-start.5
  0.0 0.0 copy-start.1
  0.0 0.0 copy-start.4
  0.0 0.0 copy-start.3
  0.0 0.0 copy-start.2
  0.0 1.4 %edges.1 = (bf16[64,1024]{1,0:T(8,128)(2,1)S(1)}, bf16[64,1024]{1,0:T(8,128)(2,1)S(1)}, bf16[16,1024]{1,0:T(8,128)(2,1)S(1)}, bf16[16,1024]{1,0:T(8,128)(2,1)S(1)}) custom-call(bf16[16,64,1024]{2,1,0:T(8,128)(2,1)} %refs_5_.3), custom_call_target="tpu_custom_call" | custom-call | tf_op jit(solution)/shard_map/edges/pallas_call | solution.py:377
  1.5 2.0 %collective-permute-start = (bf16[64,1024]{1,0:T(8,128)(2,1)S(1)}, bf16[64,1024]{1,0:T(8,128)(2,1)S(1)}, u32[]{:S(2)}, u32[]{:S(2)}) collective-permute-start(bf16[64,1024]{1,0:T(8,128)(2,1)S(1)} %get-tuple-element.20), channel_id=1, source_target_pairs={{0,8},{8,0},{16,24},{24,16},{32,40},{40,32},{48,56},{56,48},{64,72... | collective-permute-start | bytes 393224 | tf_op jit(solution)/shard_map/ppermute | solution.py:396
  3.5 7.4 %collective-permute-start.1 = (bf16[64,1024]{1,0:T(8,128)(2,1)S(1)}, bf16[64,1024]{1,0:T(8,128)(2,1)S(1)}, u32[]{:S(2)}, u32[]{:S(2)}) collective-permute-start(bf16[64,1024]{1,0:T(8,128)(2,1)S(1)} %get-tuple-element.21), channel_id=1, source_target_pairs={{0,248},{8,16},{16,8},{24,32},{32,24},{40,48},{48,40},{56,64},{64,... | collective-permute-start | bytes 393224 | tf_op jit(solution)/shard_map/ppermute | solution.py:396
  10.9 0.0 collective-permute-start.2
  10.9 0.6 %collective-permute-start.3 = (bf16[16,1024]{1,0:T(8,128)(2,1)S(1)}, bf16[16,1024]{1,0:T(8,128)(2,1)S(1)}, u32[]{:S(2)}, u32[]{:S(2)}) collective-permute-start(bf16[16,1024]{1,0:T(8,128)(2,1)S(1)} %get-tuple-element.23), channel_id=1, source_target_pairs={{0,7},{1,2},{2,1},{3,4},{4,3},{5,6},{6,5},{7,0},{8,15},{9,10},{10,... | collective-permute-start | bytes 98312 | tf_op jit(solution)/shard_map/ppermute | solution.py:396
  11.5 0.0 copy-done
  11.5 0.0 copy-done.5
  11.5 0.0 copy-done.1
  11.5 0.0 copy-done.4
  11.6 0.0 copy-done.3
  11.6 0.0 copy-done.2
  11.6 4.1 %early.1.refs_10_ = f32[8,4,24,128]{3,2,1,0:T(8,128)S(1)} custom-call(f32[4]{0:T(128)S(1)} %copy-done.2, f32[4]{0:T(128)S(1)} %copy-done.3, f32[4]{0:T(128)S(1)} %copy-done.4, f32[3,4]{1,0:T(4,128)S(1)} %copy-done.1, f32[3]{0:T(128)S(1)} %copy-done.5, bf16[16,64,1024]{2,1,0:T(8,128)(2,1)S(1)} %copy-done), custom_call_target="tpu_custom_call" | custom-call | flops 30000000 | bytes 3000000 | tf_op jit(solution)/shard_map/early/pallas_call | solution.py:406
  15.7 0.0 collective-permute-done.2.refs_8_
  15.7 0.0 collective-permute-done.3.refs_9_
  15.7 0.0 collective-permute-done.refs_6_
  15.7 0.0 collective-permute-done.1.refs_7_
  15.8 2.7 %send.1 = bf16[8,4,32,128]{3,2,1,0:T(8,128)(2,1)S(1)} custom-call(f32[4]{0:T(128)S(1)} %copy-done.2, f32[4]{0:T(128)S(1)} %copy-done.3, f32[4]{0:T(128)S(1)} %copy-done.4, f32[3,4]{1,0:T(4,128)S(1)} %copy-done.1, f32[3]{0:T(128)S(1)} %copy-done.5, bf16[16,64,1024]{2,1,0:T(8,128)(2,1)S(1)} %copy-done, bf16[64,1024]{1,0:T(8,128)(2,1)S(1)} %collective-permute-done.refs_6_, ...), custom_call_target="tpu_custom_call" | custom-call | tf_op jit(solution)/shard_map/send/pallas_call | solution.py:418
  18.5 0.1 collective-permute-start.4
  18.6 6.1 %keep.1.own = f32[8,4,32,128]{3,2,1,0:T(8,128)S(1)} custom-call(f32[4]{0:T(128)S(1)} %copy-done.2, f32[4]{0:T(128)S(1)} %copy-done.3, f32[4]{0:T(128)S(1)} %copy-done.4, f32[3,4]{1,0:T(4,128)S(1)} %copy-done.1, f32[3]{0:T(128)S(1)} %copy-done.5, bf16[16,64,1024]{2,1,0:T(8,128)(2,1)S(1)} %copy-done, bf16[64,1024]{1,0:T(8,128)(2,1)S(1)} %collective-permute-done.refs_6_, ...), custom_call_target="tpu_custom_call" | custom-call | flops 50000000 | bytes 3000000 | tf_op jit(solution)/shard_map/keep/pallas_call | solution.py:429
  24.7 3.1 %collective-permute-done.4.other = bf16[8,4,32,128]{3,2,1,0:T(8,128)(2,1)S(1)} collective-permute-done((bf16[8,4,32,128]{3,2,1,0:T(8,128)(2,1)S(1)}, bf16[8,4,32,128]{3,2,1,0:T(8,128)(2,1)S(1)}, u32[]{:S(2)}, u32[]{:S(2)}) %collective-permute-start.4) | collective-permute-done | bytes 262176 | tf_op jit(solution)/shard_map/ppermute | solution.py:428
  27.7 0.4 join.1
  28.1 16.3 %all_to_all.5.bricks = bf16[32,32,128]{2,1,0:T(8,128)(2,1)S(1)} all-to-all(bf16[32,32,128]{2,1,0:T(8,128)(2,1)S(1)} %join.1), channel_id=1, replica_groups=mesh['depth'=32,'rows'=8] {'depth'}, dimensions={0} | all-to-all | bytes 524288 | tf_op jit(solution)/shard_map/all_to_all | solution.py:447
  44.5 1.2 %compose.1 = f32[4,32,64]{2,1,0:T(8,128)} custom-call(bf16[32,32,128]{2,1,0:T(8,128)(2,1)S(1)} %all_to_all.5.bricks), custom_call_target="tpu_custom_call" | custom-call | tf_op jit(solution)/shard_map/compose/pallas_call | solution.py:448
Async XLA Ops:
  0.0 11.5 %copy-start = (bf16[16,64,1024]{2,1,0:T(8,128)(2,1)S(1)}, bf16[16,64,1024]{2,1,0:T(8,128)(2,1)}, u32[]{:S(2)}) copy-start(bf16[16,64,1024]{2,1,0:T(8,128)(2,1)} %refs_5_.3) | copy-start | bytes 6291460
  0.0 11.5 %copy-start.5 = (f32[3]{0:T(128)S(1)}, f32[3]{0:T(128)}, u32[]{:S(2)}) copy-start(f32[3]{0:T(128)} %refs_4_.5) | copy-start | bytes 40
  0.0 11.5 %copy-start.1 = (f32[3,4]{1,0:T(4,128)S(1)}, f32[3,4]{1,0:T(4,128)}, u32[]{:S(2)}) copy-start(f32[3,4]{1,0:T(4,128)} %refs_3_.5) | copy-start | bytes 148
  0.0 11.5 %copy-start.4 = (f32[4]{0:T(128)S(1)}, f32[4]{0:T(128)}, u32[]{:S(2)}) copy-start(f32[4]{0:T(128)} %refs_2_.5) | copy-start | bytes 52
  0.0 11.5 %copy-start.3 = (f32[4]{0:T(128)S(1)}, f32[4]{0:T(128)}, u32[]{:S(2)}) copy-start(f32[4]{0:T(128)} %refs_1_.5) | copy-start | bytes 52
  0.0 11.5 %copy-start.2 = (f32[4]{0:T(128)S(1)}, f32[4]{0:T(128)}, u32[]{:S(2)}) copy-start(f32[4]{0:T(128)} %refs_0_.5) | copy-start | bytes 52
  1.5 14.2 %collective-permute-start = (bf16[64,1024]{1,0:T(8,128)(2,1)S(1)}, bf16[64,1024]{1,0:T(8,128)(2,1)S(1)}, u32[]{:S(2)}, u32[]{:S(2)}) collective-permute-start(bf16[64,1024]{1,0:T(8,128)(2,1)S(1)} %get-tuple-element.20), channel_id=1, source_target_pairs={{0,8},{8,0},{16,24},{24,16},{32,40},{40,32},{48,56},{56,48},{64,72... | collective-permute-start | bytes 393224 | tf_op jit(solution)/shard_map/ppermute | solution.py:396
  3.5 12.3 %collective-permute-start.1 = (bf16[64,1024]{1,0:T(8,128)(2,1)S(1)}, bf16[64,1024]{1,0:T(8,128)(2,1)S(1)}, u32[]{:S(2)}, u32[]{:S(2)}) collective-permute-start(bf16[64,1024]{1,0:T(8,128)(2,1)S(1)} %get-tuple-element.21), channel_id=1, source_target_pairs={{0,248},{8,16},{16,8},{24,32},{32,24},{40,48},{48,40},{56,64},{64,... | collective-permute-start | bytes 393224 | tf_op jit(solution)/shard_map/ppermute | solution.py:396
  10.9 4.8 %collective-permute-start.2 = (bf16[16,1024]{1,0:T(8,128)(2,1)S(1)}, bf16[16,1024]{1,0:T(8,128)(2,1)S(1)}, u32[]{:S(2)}, u32[]{:S(2)}) collective-permute-start(bf16[16,1024]{1,0:T(8,128)(2,1)S(1)} %get-tuple-element.22), channel_id=1, source_target_pairs={{0,1},{1,0},{2,3},{3,2},{4,5},{5,4},{6,7},{7,6},{8,9},{9,8},{10,11... | collective-permute-start | bytes 98312 | tf_op jit(solution)/shard_map/ppermute | solution.py:396
  10.9 4.8 %collective-permute-start.3 = (bf16[16,1024]{1,0:T(8,128)(2,1)S(1)}, bf16[16,1024]{1,0:T(8,128)(2,1)S(1)}, u32[]{:S(2)}, u32[]{:S(2)}) collective-permute-start(bf16[16,1024]{1,0:T(8,128)(2,1)S(1)} %get-tuple-element.23), channel_id=1, source_target_pairs={{0,7},{1,2},{2,1},{3,4},{4,3},{5,6},{6,5},{7,0},{8,15},{9,10},{10,... | collective-permute-start | bytes 98312 | tf_op jit(solution)/shard_map/ppermute | solution.py:396
  18.5 9.3 %collective-permute-start.4 = (bf16[8,4,32,128]{3,2,1,0:T(8,128)(2,1)S(1)}, bf16[8,4,32,128]{3,2,1,0:T(8,128)(2,1)S(1)}, u32[]{:S(2)}, u32[]{:S(2)}) collective-permute-start(bf16[8,4,32,128]{3,2,1,0:T(8,128)(2,1)S(1)} %send.1), channel_id=1, source_target_pairs={{0,8},{8,0},{16,24},{24,16},{32,40},{40,32},{48,56},{56,48},{64,72... | collective-permute-start | bytes 786440 | tf_op jit(solution)/shard_map/ppermute | solution.py:428
